TPU v7x, 32 devices: a whole 2x2x4 slice. The times are simulated.
32 devices in a mesh: rep: 8 (over z, y), tp: 4 (over x, core).
Axes of the slice: x: 2, y: 2, z: 4, core: 2. Of those that a mesh axis runs over, the one named last changes fastest.
Arguments:
- reference_rows: bfloat16 [2048, 8192], P('rep', 'tp'), may hold values from -7 to 7
- critic_rows: bfloat16 [2048, 4096], P('rep', 'tp'), may hold values from -7 to 7
- segment_ids: int32 [2048], P('rep'), may hold values from -1 to 2047, as said below
- pack_dest: int32 [8, 8], P('rep'), may hold values from 0 to 7, as said below
- ref_query: bfloat16 [8192, 4096], P('rep', 'tp'), may hold values from -2 to 2
- ref_key: bfloat16 [8192, 1024], P('rep', 'tp'), may hold values from -2 to 2
- ref_value: bfloat16 [8192, 1024], P('rep', 'tp'), may hold values from -0.0625 to 0.0625
- critic_query: bfloat16 [4096, 4096], P(None, 'tp'), may hold values from -2 to 2
- critic_key: bfloat16 [4096, 1024], P(None, 'tp'), may hold values from -2 to 2
- critic_value: bfloat16 [4096, 1024], P(None, 'tp'), may hold values from -0.09375 to 0.09375
- ref_readout: bfloat16 [4096], P('tp'), may hold values from -0.09375 to 0.09375
- critic_readout: bfloat16 [4096], P('tp'), may hold values from -0.09375 to 0.09375
Outputs:
- ref_score: float32 [2048], P('rep')
- value: float32 [2048], P('rep')
Inputs may be any that keep to these rules, and one draw needn't show every extreme that they name: Each row is a permutation: block b of replica s goes to pack pack_dest[s, b]. `segment_ids`: in every aligned block of 32 slots the used rows come first and the rest hold -1; a block holds 1 to 31 used rows, and every pack receives exactly 31 used rows from some replica and exactly 128 used rows in all. A rollout is a run of consecutive used rows with one id inside one block; different rollouts have different ids.
All inputs are finite; a program needn't handle non-finite values.
Results may differ from a plain program's by a relative error of at most 0.0084.
Values may be sent and summed in bfloat16 or wider, within the bound.
A program may use at most 128 MiB of HBM per device.

v0:
```python
import jax
import jax.numpy as jnp
from jax import lax
from jax.sharding import PartitionSpec as P

HD = 128


def normalize(source):
    widened = source.astype(jnp.float32)
    scale_row = lax.rsqrt(jnp.mean(widened * widened, axis=-1, keepdims=True) + 1e-05)
    return (widened * scale_row).astype(jnp.bfloat16)


def attend(queries, keys_in, values_in, segments):
    row_count = queries.shape[0]
    groups = keys_in.shape[1] // HD
    shared = queries.shape[1] // keys_in.shape[1]
    query_four = queries.reshape(row_count, groups, shared, HD)
    key_three = keys_in.reshape(row_count, groups, HD)
    value_three = values_in.reshape(row_count, groups, HD)
    scores = jnp.einsum(
        "pgjd,qgd->gjpq", query_four, key_three, preferred_element_type=jnp.float32
    ) * HD ** (-0.5)
    position = jnp.arange(row_count)
    allowed = (position[None, :] <= position[:, None]) & (segments[:, None] == segments[None, :])
    masked = jnp.where(allowed, scores, -1e30)
    row_max = jnp.max(masked, axis=-1, keepdims=True)
    powers = jnp.where(allowed, jnp.exp(masked - row_max), 0.0)
    weights = (powers / jnp.sum(powers, axis=-1, keepdims=True)).astype(jnp.bfloat16)
    mixture = jnp.einsum("gjpq,qgd->pgjd", weights, value_three, preferred_element_type=jnp.float32)
    return mixture.reshape(row_count, groups * shared * HD).astype(jnp.bfloat16)


def compact_index(segments):
    row_count = segments.shape[0]
    sort_keys = jnp.where(segments >= 0, 0, row_count).astype(jnp.int32) + jnp.arange(
        row_count, dtype=jnp.int32
    )
    return jnp.argsort(sort_keys)[: row_count // 2]


def project(normed, weight):
    return jnp.dot(normed, weight, preferred_element_type=jnp.float32).astype(jnp.bfloat16)


def body(
    reference_rows,
    critic_rows,
    segment_ids,
    pack_dest,
    ref_query,
    ref_key,
    ref_value,
    critic_query,
    critic_key,
    critic_value,
    ref_readout,
    critic_readout,
):
    replicas = lax.axis_size("rep")
    slot_count = segment_ids.shape[0]
    block_rows = slot_count // replicas
    destination = pack_dest[0]
    inverse = jnp.argsort(destination)

    def by_pack(source):
        blocks = source.reshape((replicas, block_rows) + source.shape[1:])
        return jnp.take(blocks, inverse, axis=0).reshape(source.shape)

    ref_in, critic_in, ids_in = (
        lax.all_to_all(by_pack(reference_rows), "rep", split_axis=0, concat_axis=0, tiled=True),
        lax.all_to_all(by_pack(critic_rows), "rep", split_axis=0, concat_axis=0, tiled=True),
        lax.all_to_all(by_pack(segment_ids), "rep", split_axis=0, concat_axis=0, tiled=True),
    )
    chosen = compact_index(ids_in)
    pack_ids = ids_in[chosen]
    ref_full, critic_full = (
        lax.all_gather(ref_in[chosen], "tp", axis=1, tiled=True),
        lax.all_gather(critic_in[chosen], "tp", axis=1, tiled=True),
    )
    critic_normed = normalize(critic_full)
    critic_attn = attend(
        project(critic_normed, critic_query),
        project(critic_normed, critic_key),
        project(critic_normed, critic_value),
        pack_ids,
    )
    ref_normed = normalize(ref_full)
    pieces = (
        lax.all_gather(ref_query, "rep", axis=0, tiled=True),
        lax.all_gather(ref_key, "rep", axis=0, tiled=True),
        lax.all_gather(ref_value, "rep", axis=0, tiled=True),
    )
    ref_q, ref_k, ref_v = tuple(
        (
            jnp.dot(ref_normed, weight_piece, preferred_element_type=jnp.float32)
            for weight_piece in pieces
        )
    )
    ref_attn = attend(
        ref_q.astype(jnp.bfloat16), ref_k.astype(jnp.bfloat16), ref_v.astype(jnp.bfloat16), pack_ids
    )
    ref_spread = jnp.zeros((slot_count, ref_attn.shape[1]), jnp.bfloat16).at[chosen].set(ref_attn)
    critic_spread = (
        jnp.zeros((slot_count, critic_attn.shape[1]), jnp.bfloat16).at[chosen].set(critic_attn)
    )
    ref_home, critic_home = (
        lax.all_to_all(ref_spread, "rep", split_axis=0, concat_axis=0, tiled=True),
        lax.all_to_all(critic_spread, "rep", split_axis=0, concat_axis=0, tiled=True),
    )
    ref_home = jnp.take(ref_home.reshape(replicas, block_rows, -1), destination, axis=0).reshape(
        slot_count, -1
    )
    critic_home = jnp.take(
        critic_home.reshape(replicas, block_rows, -1), destination, axis=0
    ).reshape(slot_count, -1)
    partial_value = jnp.stack(
        [
            jnp.dot(ref_home, ref_readout, preferred_element_type=jnp.float32),
            jnp.dot(critic_home, critic_readout, preferred_element_type=jnp.float32),
        ]
    )
    ordered = lax.psum(partial_value, "tp")
    ordered = jnp.where(segment_ids[None, :] >= 0, ordered, 0.0)
    return (ordered[0], ordered[1])


def solution(mesh):
    return jax.shard_map(
        body,
        mesh=mesh,
        in_specs=(
            P("rep", "tp"),
            P("rep", "tp"),
            P("rep"),
            P("rep", None),
            P("rep", "tp"),
            P("rep", "tp"),
            P("rep", "tp"),
            P(None, "tp"),
            P(None, "tp"),
            P(None, "tp"),
            P("tp"),
            P("tp"),
        ),
        out_specs=(P("rep"), P("rep")),
        check_vma=False,
    )
```

profile of v0, /device:TPU:0, one launch (start us, length us, event | category | flops | bytes accessed | tf_op | source)
XLA Modules:
  0.0 520.1 jit_solution(5665056328329220842)
XLA Ops:
  10.9 7.3 %all-to-all-start = ((s32[8,32,1]{1,2,0:T(1,128)}), s32[8,32,1]{1,2,0:T(1,128)S(1)}, u32[]{:S(2)}, u32[]{:S(2)}) async-start(s32[8,32,1]{1,2,0:T(1,128)} %bitcast.2), calls=%async_computation | async-start | bytes 8192 | tf_op jit(solution)/shard_map/all_to_all | solution.py:74
  20.8 3.9 all-to-all-done
  24.7 3.5 all-to-all-start.3
  28.2 2.8 gather_fusion.1
  31.0 2.4 broadcast_select_fusion
  34.7 3.2 sort.35
  37.8 3.6 all-to-all-done.3
  42.3 3.7 all-to-all-start.1
  46.5 2.9 gather_fusion.4
  49.4 21.8 %all-to-all-done.1 = bf16[8,32,2048]{2,1,0:T(8,128)(2,1)S(1)} async-done(((bf16[8,32,2048]{2,1,0:T(8,128)(2,1)}), bf16[8,32,2048]{2,1,0:T(8,128)(2,1)S(1)}, u32[]{:S(2)}, u32[]{:S(2)}) %all-to-all-start.1) | async-done | bytes 1048608 | tf_op jit(solution)/shard_map/all_to_all | solution.py:72
  79.8 4.7 convolution_convert_fusion.1
  85.4 2.1 convolution_convert_fusion.4
  88.7 2.1 scatter_custom_fusion.1
  90.8 3.9 all-to-all-start.4
  94.7 2.1 fusion.2
  96.8 74.0 %all-gather.8.cloned.1.call-done = bf16[8192,256]{1,0:T(8,128)(2,1)} async-done(((bf16[1024,256]{1,0:T(8,128)(2,1)}), bf16[8192,256]{1,0:T(8,128)(2,1)}) %all-gather.8.cloned.1.call-update) | async-done | bytes 4194320 | tf_op jit(solution)/shard_map/all_gather | solution.py:93
  170.8 3.6 convolution_convert_fusion.7
  174.5 70.0 %all-gather.10.cloned.1.call-done = bf16[8192,256]{1,0:T(8,128)(2,1)} async-done(((bf16[1024,256]{1,0:T(8,128)(2,1)}), bf16[8192,256]{1,0:T(8,128)(2,1)}) %all-gather.10.cloned.1.call-update) | async-done | bytes 4194320 | tf_op jit(solution)/shard_map/all_gather | solution.py:92
  244.5 3.6 convolution_convert_fusion.6
  248.1 224.3 %all-gather.12.cloned.1.call-done = bf16[8192,1024]{1,0:T(8,128)(2,1)} async-done(((bf16[1024,1024]{1,0:T(8,128)(2,1)}), bf16[8192,1024]{1,0:T(8,128)(2,1)}) %all-gather.12.cloned.1.call-update) | async-done | bytes 16777232 | tf_op jit(solution)/shard_map/all_gather | solution.py:91
  472.4 8.8 %convolution_convert_fusion.3 = bf16[128,1024]{1,0:T(8,128)(2,1)S(1)} fusion(bf16[8192,1024]{1,0:T(8,128)(2,1)} %all-gather.12.cloned.1.call-done, bf16[128,8192]{1,0:T(8,128)(2,1)} %all-gather.14.cloned.1.call-done, f32[128]{0:T(128)S(1)} %add_rsqrt_fusion.1), kind=kOutput, calls=%fused_computation.35 | convolution fusion | flops 2150760448 | bytes 19137024 | tf_op jit(solution)/shard_map/dot_general | solution.py:97
  486.5 4.1 all-to-all-start.2
  491.4 13.6 %all-to-all-done.2 = bf16[8,32,1024]{2,1,0:T(8,128)(2,1)} async-done(((bf16[8,32,1024]{2,1,0:T(8,128)(2,1)}), bf16[8,32,1024]{2,1,0:T(8,128)(2,1)}, u32[]{:S(2)}, u32[]{:S(2)}) %all-to-all-start.2) | async-done | bytes 524320 | tf_op jit(solution)/shard_map/all_to_all | solution.py:109
  507.3 5.7 %psum.7 = f32[2,256]{1,0:T(2,128)S(1)} all-reduce(f32[2,256]{1,0:T(2,128)S(1)} %pad_maximum_fusion), channel_id=1, replica_groups=mesh['rep'=8,'tp'=4] {'tp'}, use_global_device_ids=true, to_apply=%region_10.12 | all-reduce | flops 512 | bytes 4096 | tf_op jit(solution)/shard_map/psum | solution.py:124
  (86 shorter events, 28.4 us)
Async XLA Ops:
  7.2 70.7 %copy-start = (bf16[4096,256]{1,0:T(8,128)(2,1)S(1)}, bf16[4096,256]{1,0:T(8,128)(2,1)}, u32[]{:S(2)}) copy-start(bf16[4096,256]{1,0:T(8,128)(2,1)} %param.23) | copy-start | bytes 6291460
  10.9 13.7 %all-to-all-start = ((s32[8,32,1]{1,2,0:T(1,128)}), s32[8,32,1]{1,2,0:T(1,128)S(1)}, u32[]{:S(2)}, u32[]{:S(2)}) async-start(s32[8,32,1]{1,2,0:T(1,128)} %bitcast.2), calls=%async_computation | async-start | bytes 8192 | tf_op jit(solution)/shard_map/all_to_all | solution.py:74
  24.7 16.7 %all-to-all-start.3 = ((bf16[8,32,1024]{2,1,0:T(8,128)(2,1)}), bf16[8,32,1024]{2,1,0:T(8,128)(2,1)S(1)}, u32[]{:S(2)}, u32[]{:S(2)}) async-start(bf16[8,32,1024]{2,1,0:T(8,128)(2,1)} %broadcast_select_fusion.1), calls=%async_computation.3 | async-start | bytes 1048576 | tf_op jit(solution)/shard_map/all_to_all | solution.py:73
  41.4 0.8 copy-start.1
  42.3 29.0 %all-to-all-start.1 = ((bf16[8,32,2048]{2,1,0:T(8,128)(2,1)}), bf16[8,32,2048]{2,1,0:T(8,128)(2,1)S(1)}, u32[]{:S(2)}, u32[]{:S(2)}) async-start(bf16[8,32,2048]{2,1,0:T(8,128)(2,1)} %broadcast_select_fusion), calls=%async_computation.1 | async-start | bytes 2097152 | tf_op jit(solution)/shard_map/all_to_all | solution.py:72
  45.9 30.3 %all-gather.16.cloned.1.call-start = ((), (), s32[]{:S(2)}) async-start(), calls=%async_computation.9 | async-start | bytes 1310720 | tf_op jit(solution)/shard_map/all_gather | solution.py:80
  46.0 0.5 copy-start.8
  49.4 45.3 %all-gather.14.cloned.1.call-start = ((), (), s32[]{:S(2)}) async-start(), calls=%async_computation.8 | async-start | bytes 2621440 | tf_op jit(solution)/shard_map/all_gather | solution.py:79
  73.0 97.8 %all-gather.8.cloned.1.call-start = ((), (), s32[]{:S(2)}) async-start(), calls=%async_computation.5 | async-start | bytes 4718592 | tf_op jit(solution)/shard_map/all_gather | solution.py:93
  73.7 170.8 %all-gather.10.cloned.1.call-start = ((), (), s32[]{:S(2)}) async-start(), calls=%async_computation.6 | async-start | bytes 4718592 | tf_op jit(solution)/shard_map/all_gather | solution.py:92
  74.3 398.1 %all-gather.12.cloned.1.call-start = ((), (), s32[]{:S(2)}) async-start(), calls=%async_computation.7 | async-start | bytes 18874368 | tf_op jit(solution)/shard_map/all_gather | solution.py:91
  76.3 3.6 copy-start.2
  77.9 6.6 %copy-start.4 = (f32[128]{0:T(128)}, f32[128]{0:T(128)S(1)}, u32[]{:S(2)}) copy-start(f32[128]{0:T(128)S(1)} %add_rsqrt_fusion) | copy-start | bytes 1540
  85.4 2.2 copy-start.3
  90.8 395.7 %all-to-all-start.4 = ((bf16[8,32,1024]{2,1,0:T(8,128)(2,1)}), bf16[8,32,1024]{2,1,0:T(8,128)(2,1)S(1)}, u32[]{:S(2)}, u32[]{:S(2)}) async-start(bf16[8,32,1024]{2,1,0:T(8,128)(2,1)} %bitcast.24), calls=%async_computation.4 | async-start | bytes 1048576 | tf_op jit(solution)/shard_map/all_to_all | solution.py:110
  482.7 8.0 %copy-start.5 = (bf16[1024]{0:T(1024)(128)(2,1)S(1)}, bf16[1024]{0:T(1024)(128)(2,1)}, u32[]{:S(2)}) copy-start(bf16[1024]{0:T(1024)(128)(2,1)} %param.25) | copy-start | bytes 6148
  482.7 8.0 %copy-start.6 = (bf16[1024]{0:T(1024)(128)(2,1)S(1)}, bf16[1024]{0:T(1024)(128)(2,1)}, u32[]{:S(2)}) copy-start(bf16[1024]{0:T(1024)(128)(2,1)} %param.24) | copy-start | bytes 6148
  482.7 8.0 %copy-start.9 = (s32[1,8]{1,0:T(1,128)S(1)}, s32[1,8]{1,0:T(1,128)}, u32[]{:S(2)}) copy-start(s32[1,8]{1,0:T(1,128)} %param.17) | copy-start | bytes 100
  482.7 8.1 %copy-start.7 = (s32[256]{0:T(256)S(1)}, s32[256]{0:T(256)}, u32[]{:S(2)}) copy-start(s32[256]{0:T(256)} %param.16) | copy-start | bytes 3076
  486.5 18.5 %all-to-all-start.2 = ((bf16[8,32,1024]{2,1,0:T(8,128)(2,1)}), bf16[8,32,1024]{2,1,0:T(8,128)(2,1)}, u32[]{:S(2)}, u32[]{:S(2)}) async-start(bf16[8,32,1024]{2,1,0:T(8,128)(2,1)} %bitcast.12), calls=%async_computation.2 | async-start | bytes 1048576 | tf_op jit(solution)/shard_map/all_to_all | solution.py:109
Sparse Core Ops, SparseCore 0:
  49.5 18.0 all-gather.15
  73.1 21.3 all-gather.13
  96.6 74.1 all-gather.7
  172.8 71.6 all-gather.9
  246.4 225.8 all-gather.11
where the time goes:
time: 521 us; the launch traced here: 520 us
  waiting for transfers between devices  413 us (79%)
  matrix products  28.9 us (6%)
  starting transfers between devices  22.7 us (4%)
  local copies, waits for them, and re-layouts  22.1 us (4%)
  between operations  14.2 us (3%)
  other arithmetic  13.6 us (3%)
  blocking collectives  5.67 us (1%)
    all_gather x1, waiting for transfers between devices, body(): lax.all_gather(ref_query, 'rep', axis=0, tiled=True)  224 us
    all_gather x1, waiting for transfers between devices, body(): lax.all_gather(ref_value, 'rep', axis=0, tiled=True)  74 us
    all_gather x1, waiting for transfers between devices, body(): lax.all_gather(ref_key, 'rep', axis=0, tiled=True)  70 us
    all_to_all x1, waiting for transfers between devices, body(): lax.all_to_all(by_pack(reference_rows), 'rep', split_axis=0, concat_axis=...  21.8 us
    dot_general x3, matrix products, body(): jnp.dot(ref_normed, weight_piece, preferred_element_type=jnp.float32)  15.9 us
    all_to_all x1, waiting for transfers between devices, body(): lax.all_to_all(ref_spread, 'rep', split_axis=0, concat_axis=0, tiled=True)  13.6 us
  transfers between devices with their start and end apart: 10, of which 7 were waited for; matrix products, arithmetic and copies ran while one was open for 11% of the time, Pallas kernels for 0%

commit v1 on v0

v1 whole, which is shorter than its diff:
```python
import jax
import jax.numpy as jnp
from jax import lax
from jax.sharding import PartitionSpec as P

HD = 128


def attend(queries, keys_in, values_in, segments):
    row_count = queries.shape[0]
    groups = keys_in.shape[1] // HD
    shared = queries.shape[1] // keys_in.shape[1]
    query_four = queries.reshape(row_count, groups, shared, HD)
    key_three = keys_in.reshape(row_count, groups, HD)
    value_three = values_in.reshape(row_count, groups, HD)
    scores = jnp.einsum(
        "pgjd,qgd->gjpq", query_four, key_three, preferred_element_type=jnp.float32
    ) * HD ** (-0.5)
    position = jnp.arange(row_count)
    allowed = (position[None, :] <= position[:, None]) & (segments[:, None] == segments[None, :])
    masked = jnp.where(allowed, scores, -1e30)
    row_max = jnp.max(masked, axis=-1, keepdims=True)
    powers = jnp.where(allowed, jnp.exp(masked - row_max), 0.0)
    weights = (powers / jnp.sum(powers, axis=-1, keepdims=True)).astype(jnp.bfloat16)
    mixture = jnp.einsum("gjpq,qgd->pgjd", weights, value_three, preferred_element_type=jnp.float32)
    return mixture.reshape(row_count, groups * shared * HD).astype(jnp.bfloat16)


def project(rows, weight):
    return jnp.dot(rows, weight, preferred_element_type=jnp.float32)


def tables(ids_all, dest_all):
    replicas = dest_all.shape[0]
    goes = dest_all[:, :, None] == jnp.arange(replicas)[None, None, :]
    inverse = jnp.sum(jnp.where(goes, jnp.arange(replicas)[None, :, None], 0), axis=1)
    ids_blocks = ids_all.reshape(replicas, replicas, -1)
    received = jnp.sum(
        jnp.where(goes[:, :, :, None], ids_blocks[:, :, None, :], 0), axis=1
    )
    received = jnp.transpose(received, (1, 0, 2)).reshape(replicas, -1)
    valid = received >= 0
    rank = jnp.cumsum(valid.astype(jnp.int32), axis=1) - 1
    return inverse, received, valid, rank


def body(
    reference_rows,
    critic_rows,
    segment_ids,
    pack_dest,
    ref_query,
    ref_key,
    ref_value,
    critic_query,
    critic_key,
    critic_value,
    ref_readout,
    critic_readout,
):
    replicas = lax.axis_size("rep")
    width = lax.axis_size("tp")
    me = lax.axis_index("rep")
    slot_count = segment_ids.shape[0]
    block_rows = slot_count // replicas
    rows_per_pack = slot_count // 2
    quarter = slot_count // width
    destination = pack_dest[0]

    info = lax.all_gather(jnp.concatenate([segment_ids, destination]), "rep", axis=0, tiled=False)
    wide_ref = reference_rows.astype(jnp.float32)
    squares = lax.all_gather(jnp.sum(wide_ref * wide_ref, axis=1), ("rep", "tp"), axis=0, tiled=False)

    split = lax.all_to_all(reference_rows, "tp", split_axis=0, concat_axis=1, tiled=True)
    slices = lax.all_to_all(split, "rep", split_axis=1, concat_axis=0, tiled=True)
    ref_slice = lax.all_gather(slices, "tp", axis=0, tiled=True)

    own_inverse = jnp.sum(
        jnp.where(
            destination[:, None] == jnp.arange(replicas)[None, :], jnp.arange(replicas)[:, None], 0
        ),
        axis=0,
    )
    blocks = critic_rows.reshape(replicas, block_rows, -1)
    critic_sent = jnp.take(blocks, own_inverse, axis=0).reshape(critic_rows.shape)
    critic_in = lax.all_to_all(critic_sent, "rep", split_axis=0, concat_axis=0, tiled=True)

    ids_all, dest_all = info[:, :slot_count], info[:, slot_count:]
    inverse, received, valid, rank = tables(ids_all, dest_all)
    place = (rank[:, None, :] == jnp.arange(rows_per_pack)[None, :, None]) & valid[:, None, :]
    position = jnp.arange(slot_count)
    sender = position // block_rows
    in_sender = jnp.transpose(inverse)[:, :, None] * block_rows + jnp.arange(block_rows)[None, None, :]
    in_sender = in_sender.reshape(replicas, slot_count)
    row_of = (in_sender // quarter) * (replicas * quarter) + sender[None, :] * quarter + in_sender % quarter
    order = jnp.sum(jnp.where(place, row_of[:, None, :], 0), axis=2).reshape(-1)

    mine = lambda table: lax.dynamic_index_in_dim(table, me, 0, keepdims=False)
    place_mine = mine(place)
    chosen = jnp.sum(jnp.where(place_mine, position[None, :], 0), axis=1)
    pack_ids = jnp.sum(jnp.where(place_mine, mine(received)[None, :], 0), axis=1)

    compact = jnp.take(ref_slice, order, axis=0)
    weight = jnp.concatenate([ref_query, ref_key, ref_value], axis=1)
    partial = project(compact, weight).astype(jnp.bfloat16)
    parts = lax.all_to_all(partial, "rep", split_axis=0, concat_axis=0, tiled=True)

    critic_full = lax.all_gather(critic_in[chosen], "tp", axis=1, tiled=True)
    widened = critic_full.astype(jnp.float32)
    scale_row = lax.rsqrt(jnp.mean(widened * widened, axis=-1, keepdims=True) + 1e-05)
    critic_normed = (widened * scale_row).astype(jnp.bfloat16)
    critic_attn = attend(
        project(critic_normed, critic_query).astype(jnp.bfloat16),
        project(critic_normed, critic_key).astype(jnp.bfloat16),
        project(critic_normed, critic_value).astype(jnp.bfloat16),
        pack_ids,
    )

    mean_square = jnp.sum(squares.reshape(replicas, width, slot_count), axis=1) / (
        reference_rows.shape[1] * width
    )
    goes_here = dest_all == me
    square_in = jnp.sum(
        jnp.where(goes_here[:, :, None], mean_square.reshape(replicas, replicas, block_rows), 0.0),
        axis=1,
    ).reshape(-1)
    square_rows = jnp.sum(jnp.where(place_mine, square_in[None, :], 0.0), axis=1)
    summed = jnp.sum(parts.reshape(replicas, rows_per_pack, -1).astype(jnp.float32), axis=0)
    ref_qkv = (summed * lax.rsqrt(square_rows + 1e-05)[:, None]).astype(jnp.bfloat16)
    nq, nk = ref_query.shape[1], ref_key.shape[1]
    ref_attn = attend(ref_qkv[:, :nq], ref_qkv[:, nq : nq + nk], ref_qkv[:, nq + nk :], pack_ids)

    terms = jnp.stack(
        [
            jnp.sum(ref_attn.astype(jnp.float32) * ref_readout.astype(jnp.float32), axis=1),
            jnp.sum(critic_attn.astype(jnp.float32) * critic_readout.astype(jnp.float32), axis=1),
        ]
    )
    spread = jnp.sum(jnp.where(place_mine[None, :, :], terms[:, :, None], 0.0), axis=1)
    everyone = lax.all_gather(spread, ("rep", "tp"), axis=0, tiled=False)
    everyone = everyone.reshape(replicas, width, 2, replicas, block_rows)
    back = lax.dynamic_index_in_dim(everyone, me, 3, keepdims=False)
    back = jnp.sum(back, axis=1)
    picked = destination[:, None] == jnp.arange(replicas)[None, :]
    home = jnp.sum(
        jnp.where(picked[:, :, None, None], back[None], 0.0), axis=1
    )
    home = jnp.transpose(home, (1, 0, 2)).reshape(2, slot_count)
    home = jnp.where(segment_ids[None, :] >= 0, home, 0.0)
    return (home[0], home[1])


def solution(mesh):
    return jax.shard_map(
        body,
        mesh=mesh,
        in_specs=(
            P("rep", "tp"),
            P("rep", "tp"),
            P("rep"),
            P("rep", None),
            P("rep", "tp"),
            P("rep", "tp"),
            P("rep", "tp"),
            P(None, "tp"),
            P(None, "tp"),
            P(None, "tp"),
            P("tp"),
            P("tp"),
        ),
        out_specs=(P("rep"), P("rep")),
        check_vma=False,
    )
```

time: 521 us -> 301 us (0.58)
  waiting for transfers between devices: 413 us -> 23.7 us
  blocking collectives: 5.67 us -> 207 us
  starting transfers between devices: 22.7 us -> 8.07 us
  matrix products: 28.9 us -> 18 us
    all_gather x5 -> x2, waiting for transfers between devices: 368 us -> 23.7 us  [the longest x1 23.6 us: body(): critic_full = lax.all_gather(critic_in[chosen], 'tp', axis=1, tiled=True)]
    all_gather x0 -> x2, blocking collectives: none -> 118 us  [the longest x1 77.6 us: body(): lax.all_gather(jnp.sum(wide_ref * wide_ref, axis=1), ('rep', 'tp'), axis=...]
    all_to_all x0 -> x2, blocking collectives: none -> 50.9 us  [the longest x1 32 us: body(): lax.all_to_all(split, 'rep', split_axis=1, concat_axis=0, tiled=True)]
    all_to_all x5 -> x2, waiting for transfers between devices: 43 us -> 0.01 us  [the longest x1 0.01 us: body(): lax.all_to_all(critic_sent, 'rep', split_axis=0, concat_axis=0, tiled=True)]
    unnamed x0 -> x1, blocking collectives: none -> 37.6 us
    all_to_all x5 -> x2, starting transfers between devices: 22.5 us -> 7.99 us  [the longest x1 4.44 us: body(): lax.all_to_all(partial, 'rep', split_axis=0, concat_axis=0, tiled=True)]
    dot_general x10 -> x4, matrix products: 26.3 us -> 16.7 us  [project(): return jnp.dot(rows, weight, preferred_element_type=jnp.float32)]
    psum x1 -> x0, blocking collectives: 5.67 us -> none  [body(): ordered = lax.psum(partial_value, 'tp')]
  transfers between devices with their start and end apart: 10 -> 4, of which waited for: 7 -> 1; matrix products, arithmetic and copies ran while one was open for 11% -> 13% of each run, Pallas kernels for 0% -> 0%
where the time goes in v1:
time: 301 us; the launch traced here: 300 us
  blocking collectives  207 us (69%)
  waiting for transfers between devices  23.7 us (8%)
  local copies, waits for them, and re-layouts  19.5 us (6%)
  matrix products  18 us (6%)
  between operations  15.2 us (5%)
  other arithmetic  9.26 us (3%)
  starting transfers between devices  8.07 us (3%)
    all_gather x1, blocking collectives, body(): lax.all_gather(jnp.sum(wide_ref * wide_ref, axis=1), ('rep', 'tp'), axis=...  77.6 us
    all_gather x1, blocking collectives, body(): everyone = lax.all_gather(spread, ('rep', 'tp'), axis=0, tiled=False)  40.7 us
    unnamed x1, blocking collectives  37.6 us
    all_to_all x1, blocking collectives, body(): lax.all_to_all(split, 'rep', split_axis=1, concat_axis=0, tiled=True)  32 us
    all_gather x1, waiting for transfers between devices, body(): critic_full = lax.all_gather(critic_in[chosen], 'tp', axis=1, tiled=True)  23.6 us
    all_to_all x1, blocking collectives, body(): lax.all_to_all(reference_rows, 'tp', split_axis=0, concat_axis=1, tiled=T...  18.8 us
    dot_general x4, matrix products, project(): return jnp.dot(rows, weight, preferred_element_type=jnp.float32)  16.7 us
    gather x1, local copies, waits for them, and re-layouts, body(): compact = jnp.take(ref_slice, order, axis=0)  8.83 us
  transfers between devices with their start and end apart: 4, of which 1 were waited for; matrix products, arithmetic and copies ran while one was open for 13% of the time, Pallas kernels for 0%

profile of v1, /device:TPU:0, one launch (start us, length us, event | category | flops | bytes accessed | tf_op | source)
XLA Modules:
  0.0 300.4 jit_solution(2625178527744819786)
XLA Ops:
  7.2 18.8 %all_to_all.53 = bf16[4,64,2048]{2,1,0:T(8,128)(2,1)S(1)} all-to-all(bf16[4,64,2048]{2,1,0:T(8,128)(2,1)} %bitcast.102), channel_id=1, replica_groups=mesh['rep'=8,'tp'=4] {'tp'}, dimensions={0} | all-to-all | bytes 2097152 | tf_op jit(solution)/shard_map/all_to_all | solution.py:74
  26.0 0.8 copy.79
  26.9 1.1 all_to_all.41
  28.0 1.8 copy.80
  29.8 32.0 %all_to_all.54 = bf16[64,8,1024]{2,0,1:T(8,128)(2,1)} all-to-all(bf16[64,8,1024]{2,0,1:T(8,128)(2,1)S(1)} %copy.80), channel_id=1, replica_groups=mesh['rep'=8,'tp'=4] {'rep'}, dimensions={1} | all-to-all | bytes 2097152 | tf_op jit(solution)/shard_map/all_to_all | solution.py:75
  62.6 0.9 broadcast_select_fusion
  63.5 3.5 %all-to-all-start.3 = ((bf16[8,32,1024]{2,1,0:T(8,128)(2,1)}), bf16[8,32,1024]{2,1,0:T(8,128)(2,1)S(1)}, u32[]{:S(2)}, u32[]{:S(2)}) async-start(bf16[8,32,1024]{2,1,0:T(8,128)(2,1)} %broadcast_select_fusion), calls=%async_computation.3 | async-start | bytes 1048576 | tf_op jit(solution)/shard_map/all_to_all | solution.py:86
  68.5 37.6 %all-reduce = s32[2112]{0:T(1024)S(1)} all-reduce(s32[2112]{0:T(1024)S(1)} %add_dynamic-update-slice_fusion), channel_id=2, replica_groups=mesh['rep'=8,'tp'=4] {'rep'}, use_global_device_ids=true, to_apply=%add | all-reduce | flops 2112 | bytes 16896
  106.6 0.6 reduce-window.6
  108.4 8.8 %gather_fusion = bf16[1024,1024]{1,0:T(8,128)(2,1)} fusion(bf16[2048,1024]{1,0:T(8,128)(2,1)} %all-gather.9.cloned.1.call-done, s32[1024]{0:T(1024)S(1)} %broadcast_clamp_fusion), kind=kCustom, calls=%fused_computation | custom fusion | bytes 4198400 | tf_op jit(solution)/shard_map/jit(_take)/gather | solution.py:103
  117.2 7.5 %convolution_convert_fusion = bf16[1024,1536]{1,0:T(8,128)(2,1)} fusion(bf16[1024,256]{1,0:T(8,128)(2,1)S(1)} %copy-done.8, bf16[1024,256]{1,0:T(8,128)(2,1)} %param.17, bf16[1024,1024]{1,0:T(8,128)(2,1)} %param.16, bf16[1024,1024]{1,0:T(8,128)(2,1)} %gather_fusion, pred[1024]{0:T(1024)(128)(4,1)S(1)} %compare_and_fusion), kind=kOutput, calls=%fused_computation.6 | convolution fusion | flops 3233284096 | bytes 8389632 | tf_op jit(solution)/shard_map/dot_general | solution.py:30
  124.7 4.4 %all-to-all-start.2 = ((bf16[8,128,1536]{2,1,0:T(8,128)(2,1)}), bf16[8,128,1536]{2,1,0:T(8,128)(2,1)}, u32[]{:S(2)}, u32[]{:S(2)}) async-start(bf16[8,128,1536]{2,1,0:T(8,128)(2,1)} %bitcast.105), calls=%async_computation.2 | async-start | bytes 6291456 | tf_op jit(solution)/shard_map/all_to_all | solution.py:106
  129.3 1.5 multiply_reduce_fusion
  130.8 77.6 %all-gather.4 = f32[32,1,256]{2,1,0:T(1,128)S(1)} all-gather(f32[1,1,256]{2,1,0:T(1,128)S(1)} %bitcast.117), channel_id=3, replica_groups=mesh['rep'=8,'tp'=4] {'rep','tp'}, dimensions={0}, use_global_device_ids=true | all-gather | bytes 33792 | tf_op jit(solution)/shard_map/all_gather | solution.py:72
  209.2 1.6 gather_fusion.2
  211.1 23.6 %all-gather.11.cloned.1.call-done = bf16[128,4096]{1,0:T(8,128)(2,1)} async-done(((bf16[128,1024]{1,0:T(8,128)(2,1)}), bf16[128,4096]{1,0:T(8,128)(2,1)}) %all-gather.11.cloned.1.call-update) | async-done | bytes 1048592 | tf_op jit(solution)/shard_map/all_gather | solution.py:108
  234.7 1.6 fusion.7
  236.3 1.7 convolution_convert_fusion.4
  238.1 4.7 %convolution_convert_fusion.2 = bf16[128,1024]{1,0:T(8,128)(2,1)S(1)} fusion(bf16[4096,1024]{1,0:T(8,128)(2,1)} %param.19, bf16[128,4096]{1,0:T(8,128)(2,1)S(1)} %copy-done.1, f32[128]{0:T(128)S(1)} %add_rsqrt_fusion), kind=kOutput, calls=%fused_computation.35 | convolution fusion | flops 1075445760 | bytes 9699840 | tf_op jit(solution)/shard_map/dot_general | solution.py:30
  242.8 0.9 reshape.321
  243.6 2.7 convolution_convert_fusion.5
  246.4 0.9 copy.102
  248.0 2.4 convert_reduce_fusion
  251.8 40.7 %all-gather.5 = f32[32,2,256]{2,1,0:T(2,128)S(1)} all-gather(f32[1,2,256]{2,1,0:T(2,128)S(1)} %bitcast.116), channel_id=5, replica_groups=mesh['rep'=8,'tp'=4] {'rep','tp'}, dimensions={0}, use_global_device_ids=true | all-gather | bytes 67584 | tf_op jit(solution)/shard_map/all_gather | solution.py:140
  (107 shorter events, 7.2 us)
Async XLA Ops:
  7.2 229.2 %copy-start = (bf16[4096,256]{1,0:T(8,128)(2,1)S(1)}, bf16[4096,256]{1,0:T(8,128)(2,1)}, u32[]{:S(2)}) copy-start(bf16[4096,256]{1,0:T(8,128)(2,1)} %param.20) | copy-start | bytes 6291460
  7.2 101.2 %all-gather.9.cloned.1.call-start = ((), (), s32[]{:S(2)}) async-start(), calls=%async_computation.4 | async-start | bytes 5242880 | tf_op jit(solution)/shard_map/all_gather | solution.py:76
  29.8 32.1 %copy-start.7 = (s32[1,8]{1,0:T(1,128)S(1)}, s32[1,8]{1,0:T(1,128)}, u32[]{:S(2)}) copy-start(s32[1,8]{1,0:T(1,128)} %param.15) | copy-start | bytes 100
  29.8 32.2 %copy-start.2 = (bf16[256,1024]{1,0:T(8,128)(2,1)S(1)}, bf16[256,1024]{1,0:T(8,128)(2,1)}, u32[]{:S(2)}) copy-start(bf16[256,1024]{1,0:T(8,128)(2,1)} %param.13) | copy-start | bytes 1572868
  61.9 5.2 %copy-start.9 = (u32[32]{0:T(128)S(1)}, u32[32]{0:T(128)}, u32[]{:S(2)}) copy-start(u32[32]{0:T(128)} %constant.126) | copy-start | bytes 388
  61.9 6.5 %copy-start.6 = (s32[256]{0:T(256)S(1)}, s32[256]{0:T(256)}, u32[]{:S(2)}) copy-start(s32[256]{0:T(256)} %param.14) | copy-start | bytes 3076
  63.5 61.2 %all-to-all-start.3 = ((bf16[8,32,1024]{2,1,0:T(8,128)(2,1)}), bf16[8,32,1024]{2,1,0:T(8,128)(2,1)S(1)}, u32[]{:S(2)}, u32[]{:S(2)}) async-start(bf16[8,32,1024]{2,1,0:T(8,128)(2,1)} %broadcast_select_fusion), calls=%async_computation.3 | async-start | bytes 1048576 | tf_op jit(solution)/shard_map/all_to_all | solution.py:86
  108.3 8.9 %copy-start.8 = (bf16[1024,256]{1,0:T(8,128)(2,1)S(1)}, bf16[1024,256]{1,0:T(8,128)(2,1)}, u32[]{:S(2)}) copy-start(bf16[1024,256]{1,0:T(8,128)(2,1)} %param.18) | copy-start | bytes 1572868
  124.7 123.3 %all-to-all-start.2 = ((bf16[8,128,1536]{2,1,0:T(8,128)(2,1)}), bf16[8,128,1536]{2,1,0:T(8,128)(2,1)}, u32[]{:S(2)}, u32[]{:S(2)}) async-start(bf16[8,128,1536]{2,1,0:T(8,128)(2,1)} %bitcast.105), calls=%async_computation.2 | async-start | bytes 6291456 | tf_op jit(solution)/shard_map/all_to_all | solution.py:106
  129.2 105.5 %all-gather.11.cloned.1.call-start = ((), (), s32[]{:S(2)}) async-start(), calls=%async_computation.5 | async-start | bytes 1310720 | tf_op jit(solution)/shard_map/all_gather | solution.py:108
  129.2 81.6 %copy-start.4 = (bf16[1024]{0:T(1024)(128)(2,1)S(1)}, bf16[1024]{0:T(1024)(128)(2,1)}, u32[]{:S(2)}) copy-start(bf16[1024]{0:T(1024)(128)(2,1)} %param.22) | copy-start | bytes 6148
  129.3 81.6 %copy-start.5 = (bf16[1024]{0:T(1024)(128)(2,1)S(1)}, bf16[1024]{0:T(1024)(128)(2,1)}, u32[]{:S(2)}) copy-start(bf16[1024]{0:T(1024)(128)(2,1)} %param.23) | copy-start | bytes 6148
  234.7 3.4 %copy-start.1 = (bf16[128,4096]{1,0:T(8,128)(2,1)S(1)}, bf16[128,4096]{1,0:T(8,128)(2,1)}, u32[]{:S(2)}) copy-start(bf16[128,4096]{1,0:T(8,128)(2,1)} %all-gather.11.cloned.1.call-done) | copy-start | bytes 3145732
  243.6 3.7 %copy-start.3 = (bf16[128,2,4,128]{3,2,1,0:T(4,128)(2,1)S(1)}, bf16[128,2,4,128]{3,2,1,0:T(4,128)(2,1)}, u32[]{:S(2)}) copy-start(bf16[128,2,4,128]{3,2,1,0:T(4,128)(2,1)} %reshape.321) | copy-start | bytes 786436
Sparse Core Ops, SparseCore 0:
  62.0 32.7 all-gather.8
  211.0 23.6 all-gather.10

commit v2 on v1

--- a/solution.py
+++ b/solution.py
@@ -69,18 +69,23 @@
 
     info = lax.all_gather(jnp.concatenate([segment_ids, destination]), "rep", axis=0, tiled=False)
     wide_ref = reference_rows.astype(jnp.float32)
-    squares = lax.all_gather(jnp.sum(wide_ref * wide_ref, axis=1), ("rep", "tp"), axis=0, tiled=False)
-
-    split = lax.all_to_all(reference_rows, "tp", split_axis=0, concat_axis=1, tiled=True)
-    slices = lax.all_to_all(split, "rep", split_axis=1, concat_axis=0, tiled=True)
-    ref_slice = lax.all_gather(slices, "tp", axis=0, tiled=True)
-
+    squares = lax.psum(jnp.sum(wide_ref * wide_ref, axis=1), "tp")
     own_inverse = jnp.sum(
         jnp.where(
             destination[:, None] == jnp.arange(replicas)[None, :], jnp.arange(replicas)[:, None], 0
         ),
         axis=0,
     )
+    squares_sent = jnp.take(squares.reshape(replicas, block_rows), own_inverse, axis=0)
+    square_in = lax.all_to_all(squares_sent, "rep", split_axis=0, concat_axis=0, tiled=True).reshape(-1)
+    info, square_in, reference_rows, critic_rows = lax.optimization_barrier(
+        (info, square_in, reference_rows, critic_rows)
+    )
+
+    split = lax.all_to_all(reference_rows, "tp", split_axis=0, concat_axis=1, tiled=True)
+    slices = lax.all_to_all(split, "rep", split_axis=1, concat_axis=0, tiled=True)
+    ref_slice = lax.all_gather(slices, "tp", axis=0, tiled=True)
+
     blocks = critic_rows.reshape(replicas, block_rows, -1)
     critic_sent = jnp.take(blocks, own_inverse, axis=0).reshape(critic_rows.shape)
     critic_in = lax.all_to_all(critic_sent, "rep", split_axis=0, concat_axis=0, tiled=True)
@@ -116,15 +121,9 @@
         pack_ids,
     )
 
-    mean_square = jnp.sum(squares.reshape(replicas, width, slot_count), axis=1) / (
+    square_rows = jnp.sum(jnp.where(place_mine, square_in[None, :], 0.0), axis=1) / (
         reference_rows.shape[1] * width
     )
-    goes_here = dest_all == me
-    square_in = jnp.sum(
-        jnp.where(goes_here[:, :, None], mean_square.reshape(replicas, replicas, block_rows), 0.0),
-        axis=1,
-    ).reshape(-1)
-    square_rows = jnp.sum(jnp.where(place_mine, square_in[None, :], 0.0), axis=1)
     summed = jnp.sum(parts.reshape(replicas, rows_per_pack, -1).astype(jnp.float32), axis=0)
     ref_qkv = (summed * lax.rsqrt(square_rows + 1e-05)[:, None]).astype(jnp.bfloat16)
     nq, nk = ref_query.shape[1], ref_key.shape[1]
@@ -137,10 +136,10 @@
         ]
     )
     spread = jnp.sum(jnp.where(place_mine[None, :, :], terms[:, :, None], 0.0), axis=1)
-    everyone = lax.all_gather(spread, ("rep", "tp"), axis=0, tiled=False)
-    everyone = everyone.reshape(replicas, width, 2, replicas, block_rows)
-    back = lax.dynamic_index_in_dim(everyone, me, 3, keepdims=False)
-    back = jnp.sum(back, axis=1)
+    spread = lax.psum(spread, "tp").reshape(2, replicas, block_rows)
+    sent = jnp.transpose(spread, (1, 0, 2)).reshape(replicas, 2 * block_rows)
+    back = lax.all_to_all(sent, "rep", split_axis=0, concat_axis=0, tiled=True)
+    back = back.reshape(replicas, 2, block_rows)
     picked = destination[:, None] == jnp.arange(replicas)[None, :]
     home = jnp.sum(
         jnp.where(picked[:, :, None, None], back[None], 0.0), axis=1

time: 301 us -> 273 us (0.907)
  blocking collectives: 207 us -> 99.2 us
  waiting for transfers between devices: 23.7 us -> 87.5 us
  starting transfers between devices: 8.07 us -> 18.8 us
  other arithmetic: 9.26 us -> 12.5 us
    all_gather x2 -> x0, blocking collectives: 118 us -> none  [the longest x1 77.6 us: body(): lax.all_gather(jnp.sum(wide_ref * wide_ref, axis=1), ('rep', 'tp'), axis=...]
    all_to_all x1, waiting for transfers between devices: 0.01 us -> 38.2 us  [body(): lax.all_to_all(partial, 'rep', split_axis=0, concat_axis=0, tiled=True)]
    all_gather x1, waiting for transfers between devices: 0.02 us -> 25.7 us  [body(): ref_slice = lax.all_gather(slices, 'tp', axis=0, tiled=True)]
    psum x0 -> x2, blocking collectives: none -> 14.8 us  [the longest x1 8.31 us: body(): squares = lax.psum(jnp.sum(wide_ref * wide_ref, axis=1), 'tp')]
    all_to_all x0 -> x2, starting transfers between devices: none -> 9.45 us  [the longest x1 5.83 us: body(): lax.all_to_all(squares_sent, 'rep', split_axis=0, concat_axis=0, tiled=True)]
    all_gather x1, waiting for transfers between devices: 23.6 us -> 17.1 us  [body(): critic_full = lax.all_gather(critic_in[chosen], 'tp', axis=1, tiled=True)]
    all_to_all x0 -> x2, waiting for transfers between devices: none -> 6.45 us  [the longest x1 6.45 us: body(): back = lax.all_to_all(sent, 'rep', split_axis=0, concat_axis=0, tiled=True)]
    all_to_all x1, blocking collectives: 32 us -> 28.9 us  [body(): lax.all_to_all(split, 'rep', split_axis=1, concat_axis=0, tiled=True)]
  transfers between devices with their start and end apart: 4 -> 6, of which waited for: 1 -> 4; matrix products, arithmetic and copies ran while one was open for 13% -> 14% of each run, Pallas kernels for 0% -> 0%
where the time goes in v2:
time: 273 us; the launch traced here: 272 us
  blocking collectives  99.2 us (36%)
  waiting for transfers between devices  87.5 us (32%)
  local copies, waits for them, and re-layouts  21.2 us (8%)
  starting transfers between devices  18.8 us (7%)
  matrix products  18.2 us (7%)
  between operations  15.1 us (6%)
  other arithmetic  12.5 us (5%)
    all_to_all x1, waiting for transfers between devices, body(): lax.all_to_all(partial, 'rep', split_axis=0, concat_axis=0, tiled=True)  38.2 us
    unnamed x1, blocking collectives  37.5 us
    all_to_all x1, blocking collectives, body(): lax.all_to_all(split, 'rep', split_axis=1, concat_axis=0, tiled=True)  28.9 us
    all_gather x1, waiting for transfers between devices, body(): ref_slice = lax.all_gather(slices, 'tp', axis=0, tiled=True)  25.7 us
    all_to_all x1, blocking collectives, body(): lax.all_to_all(reference_rows, 'tp', split_axis=0, concat_axis=1, tiled=T...  17.9 us
    all_gather x1, waiting for transfers between devices, body(): critic_full = lax.all_gather(critic_in[chosen], 'tp', axis=1, tiled=True)  17.1 us
    dot_general x4, matrix products, project(): return jnp.dot(rows, weight, preferred_element_type=jnp.float32)  16.8 us
    gather x1, local copies, waits for them, and re-layouts, body(): compact = jnp.take(ref_slice, order, axis=0)  8.78 us
  transfers between devices with their start and end apart: 6, of which 4 were waited for; matrix products, arithmetic and copies ran while one was open for 14% of the time, Pallas kernels for 0%

profile of v2, /device:TPU:0, one launch (start us, length us, event | category | flops | bytes accessed | tf_op | source)
XLA Modules:
  0.0 272.5 jit_solution(15370445146532148663)
XLA Ops:
  8.1 1.5 multiply_reduce_fusion
  9.7 8.3 %psum.14 = f32[8,32]{1,0:T(8,128)S(1)} all-reduce(f32[8,32]{1,0:T(8,128)S(1)} %reshape.340), channel_id=1, replica_groups=mesh['rep'=8,'tp'=4] {'tp'}, use_global_device_ids=true, to_apply=%region_2.3 | all-reduce | flops 256 | bytes 2048 | tf_op jit(solution)/shard_map/psum | solution.py:72
  19.2 5.8 %all-to-all-start = ((f32[8,1,32]{2,1,0:T(1,128)}), f32[8,1,32]{2,1,0:T(1,128)S(1)}, u32[]{:S(2)}, u32[]{:S(2)}) async-start(f32[8,1,32]{2,1,0:T(1,128)} %bitcast.5), calls=%async_computation | async-start | bytes 8192 | tf_op jit(solution)/shard_map/all_to_all | solution.py:80
  25.1 1.2 dynamic-slice
  27.8 37.5 %all-reduce = s32[2112]{0:T(1024)S(1)} all-reduce(s32[2112]{0:T(1024)S(1)} %add_dynamic-update-slice_fusion), channel_id=2, replica_groups=mesh['rep'=8,'tp'=4] {'rep'}, use_global_device_ids=true, to_apply=%add | all-reduce | flops 2112 | bytes 16896
  66.7 17.9 %all_to_all.68 = bf16[4,64,2048]{2,1,0:T(8,128)(2,1)S(1)} all-to-all(bf16[4,64,2048]{2,1,0:T(8,128)(2,1)} %bitcast.105), channel_id=1, replica_groups=mesh['rep'=8,'tp'=4] {'tp'}, dimensions={0} | all-to-all | bytes 2097152 | tf_op jit(solution)/shard_map/all_to_all | solution.py:85
  86.6 1.8 copy.82
  88.4 28.9 %all_to_all.69 = bf16[64,8,1024]{2,0,1:T(8,128)(2,1)} all-to-all(bf16[64,8,1024]{2,0,1:T(8,128)(2,1)S(1)} %copy.82), channel_id=1, replica_groups=mesh['rep'=8,'tp'=4] {'rep'}, dimensions={1} | all-to-all | bytes 2097152 | tf_op jit(solution)/shard_map/all_to_all | solution.py:86
  120.6 3.6 %all-to-all-start.4 = ((bf16[8,32,1024]{2,1,0:T(8,128)(2,1)}), bf16[8,32,1024]{2,1,0:T(8,128)(2,1)S(1)}, u32[]{:S(2)}, u32[]{:S(2)}) async-start(bf16[8,32,1024]{2,1,0:T(8,128)(2,1)} %broadcast_select_fusion), calls=%async_computation.4 | async-start | bytes 1048576 | tf_op jit(solution)/shard_map/all_to_all | solution.py:91
  124.6 25.7 %all-gather.5.cloned.1.call-done = bf16[2048,1024]{1,0:T(8,128)(2,1)} async-done(((bf16[512,1024]{1,0:T(8,128)(2,1)}), bf16[2048,1024]{1,0:T(8,128)(2,1)}) %all-gather.5.cloned.1.call-update) | async-done | bytes 4194320 | tf_op jit(solution)/shard_map/all_gather | solution.py:87
  150.3 8.8 %gather_fusion.1 = bf16[1024,1024]{1,0:T(8,128)(2,1)} fusion(bf16[2048,1024]{1,0:T(8,128)(2,1)} %all-gather.5.cloned.1.call-done, s32[1024]{0:T(1024)S(1)} %broadcast_clamp_fusion), kind=kCustom, calls=%fused_computation.1 | custom fusion | bytes 4198400 | tf_op jit(solution)/shard_map/jit(_take)/gather | solution.py:108
  159.1 7.7 %convolution_convert_fusion = bf16[1024,1536]{1,0:T(8,128)(2,1)} fusion(bf16[1024,256]{1,0:T(8,128)(2,1)} %param.18, bf16[1024,256]{1,0:T(8,128)(2,1)} %param.17, bf16[1024,1024]{1,0:T(8,128)(2,1)} %param.16, bf16[1024,1024]{1,0:T(8,128)(2,1)} %gather_fusion.1, pred[1024]{0:T(1024)(128)(4,1)S(1)} %compare_and_fusion), kind=kOutput, calls=%fused_computation.7 | convolution fusion | flops 3233284096 | bytes 8389632 | tf_op jit(solution)/shard_map/dot_general | solution.py:30
  166.8 5.5 %all-to-all-start.3 = ((bf16[8,128,1536]{2,1,0:T(8,128)(2,1)}), bf16[8,128,1536]{2,1,0:T(8,128)(2,1)}, u32[]{:S(2)}, u32[]{:S(2)}) async-start(bf16[8,128,1536]{2,1,0:T(8,128)(2,1)} %bitcast.108), calls=%async_computation.3 | async-start | bytes 6291456 | tf_op jit(solution)/shard_map/all_to_all | solution.py:111
  173.0 1.6 gather_fusion.3
  174.8 17.1 %all-gather.7.cloned.1.call-done = bf16[128,4096]{1,0:T(8,128)(2,1)} async-done(((bf16[128,1024]{1,0:T(8,128)(2,1)}), bf16[128,4096]{1,0:T(8,128)(2,1)}) %all-gather.7.cloned.1.call-update) | async-done | bytes 1048592 | tf_op jit(solution)/shard_map/all_gather | solution.py:113
  192.0 1.6 fusion.7
  193.6 1.7 convolution_convert_fusion.4
  195.3 4.7 %convolution_convert_fusion.2 = bf16[128,1024]{1,0:T(8,128)(2,1)S(1)} fusion(bf16[4096,1024]{1,0:T(8,128)(2,1)} %param.19, bf16[128,4096]{1,0:T(8,128)(2,1)S(1)} %copy-done.1, f32[128]{0:T(128)S(1)} %add_rsqrt_fusion), kind=kOutput, calls=%fused_computation.36 | convolution fusion | flops 1075445760 | bytes 9699840 | tf_op jit(solution)/shard_map/dot_general | solution.py:30
  200.9 2.7 %convolution_convert_fusion.5 = bf16[128,256]{1,0:T(8,128)(2,1)} fusion(bf16[4096,256]{1,0:T(8,128)(2,1)} %param.21, bf16[128,4096]{1,0:T(8,128)(2,1)S(1)} %copy-done.1, f32[128]{0:T(128)S(1)} %add_rsqrt_fusion), kind=kOutput, calls=%fused_computation.44 | convolution fusion | flops 270041088 | bytes 3211776 | tf_op jit(solution)/shard_map/dot_general | solution.py:30
  205.3 38.2 %all-to-all-done.3 = bf16[8,128,1536]{2,1,0:T(8,128)(2,1)} async-done(((bf16[8,128,1536]{2,1,0:T(8,128)(2,1)}), bf16[8,128,1536]{2,1,0:T(8,128)(2,1)}, u32[]{:S(2)}, u32[]{:S(2)}) %all-to-all-start.3) | async-done | bytes 3145760 | tf_op jit(solution)/shard_map/all_to_all | solution.py:111
  243.5 2.4 convert_reduce_fusion
  247.5 6.5 %psum.15 = f32[8,1,64]{2,0,1:T(8,128)} all-reduce(f32[8,1,64]{2,0,1:T(8,128)S(1)} %all_to_all.60), channel_id=1, replica_groups=mesh['rep'=8,'tp'=4] {'tp'}, use_global_device_ids=true, to_apply=%region_20.21 | all-reduce | flops 512 | bytes 4096 | tf_op jit(solution)/shard_map/psum | solution.py:139
  254.0 3.6 %all-to-all-start.5 = ((f32[8,1,64]{2,1,0:T(1,128)}), f32[8,1,64]{2,1,0:T(1,128)S(1)}, u32[]{:S(2)}, u32[]{:S(2)}) async-start(f32[8,1,64]{2,1,0:T(1,128)} %bitcast.42), calls=%async_computation.5 | async-start | bytes 8192 | tf_op jit(solution)/shard_map/all_to_all | solution.py:141
  257.7 6.4 %all-to-all-done.5 = f32[8,1,64]{2,1,0:T(1,128)S(1)} async-done(((f32[8,1,64]{2,1,0:T(1,128)}), f32[8,1,64]{2,1,0:T(1,128)S(1)}, u32[]{:S(2)}, u32[]{:S(2)}) %all-to-all-start.5) | async-done | bytes 2080 | tf_op jit(solution)/shard_map/all_to_all | solution.py:141
  (108 shorter events, 16.5 us)
Async XLA Ops:
  7.2 186.4 %copy-start = (bf16[4096,256]{1,0:T(8,128)(2,1)S(1)}, bf16[4096,256]{1,0:T(8,128)(2,1)}, u32[]{:S(2)}) copy-start(bf16[4096,256]{1,0:T(8,128)(2,1)} %param.20) | copy-start | bytes 6291460
  19.2 46.2 %all-to-all-start = ((f32[8,1,32]{2,1,0:T(1,128)}), f32[8,1,32]{2,1,0:T(1,128)S(1)}, u32[]{:S(2)}, u32[]{:S(2)}) async-start(f32[8,1,32]{2,1,0:T(1,128)} %bitcast.5), calls=%async_computation | async-start | bytes 8192 | tf_op jit(solution)/shard_map/all_to_all | solution.py:80
  25.1 125.3 %all-gather.5.cloned.1.call-start = ((), (), s32[]{:S(2)}) async-start(), calls=%async_computation.6 | async-start | bytes 5242880 | tf_op jit(solution)/shard_map/all_gather | solution.py:87
  88.4 30.7 %copy-start.2 = (bf16[256,1024]{1,0:T(8,128)(2,1)S(1)}, bf16[256,1024]{1,0:T(8,128)(2,1)}, u32[]{:S(2)}) copy-start(bf16[256,1024]{1,0:T(8,128)(2,1)} %param.13) | copy-start | bytes 1572868
  120.6 46.1 %all-to-all-start.4 = ((bf16[8,32,1024]{2,1,0:T(8,128)(2,1)}), bf16[8,32,1024]{2,1,0:T(8,128)(2,1)S(1)}, u32[]{:S(2)}, u32[]{:S(2)}) async-start(bf16[8,32,1024]{2,1,0:T(8,128)(2,1)} %broadcast_select_fusion), calls=%async_computation.4 | async-start | bytes 1048576 | tf_op jit(solution)/shard_map/all_to_all | solution.py:91
  166.8 76.7 %all-to-all-start.3 = ((bf16[8,128,1536]{2,1,0:T(8,128)(2,1)}), bf16[8,128,1536]{2,1,0:T(8,128)(2,1)}, u32[]{:S(2)}, u32[]{:S(2)}) async-start(bf16[8,128,1536]{2,1,0:T(8,128)(2,1)} %bitcast.108), calls=%async_computation.3 | async-start | bytes 6291456 | tf_op jit(solution)/shard_map/all_to_all | solution.py:111
  172.3 2.3 copy-start.4
  172.3 2.3 copy-start.5
  172.3 2.4 copy-start.7
  172.3 19.6 %all-gather.7.cloned.1.call-start = ((), (), s32[]{:S(2)}) async-start(), calls=%async_computation.7 | async-start | bytes 1310720 | tf_op jit(solution)/shard_map/all_gather | solution.py:113
  192.0 3.4 %copy-start.1 = (bf16[128,4096]{1,0:T(8,128)(2,1)S(1)}, bf16[128,4096]{1,0:T(8,128)(2,1)}, u32[]{:S(2)}) copy-start(bf16[128,4096]{1,0:T(8,128)(2,1)} %all-gather.7.cloned.1.call-done) | copy-start | bytes 3145732
  200.9 3.7 %copy-start.3 = (bf16[128,2,4,128]{3,2,1,0:T(4,128)(2,1)S(1)}, bf16[128,2,4,128]{3,2,1,0:T(4,128)(2,1)}, u32[]{:S(2)}) copy-start(bf16[128,2,4,128]{3,2,1,0:T(4,128)(2,1)} %reshape.352) | copy-start | bytes 786436
  246.1 11.6 %copy-start.6 = (s32[256]{0:T(256)S(1)}, s32[256]{0:T(256)}, u32[]{:S(2)}) copy-start(s32[256]{0:T(256)} %param.14) | copy-start | bytes 3076
  254.0 10.1 %all-to-all-start.5 = ((f32[8,1,64]{2,1,0:T(1,128)}), f32[8,1,64]{2,1,0:T(1,128)S(1)}, u32[]{:S(2)}, u32[]{:S(2)}) async-start(f32[8,1,64]{2,1,0:T(1,128)} %bitcast.42), calls=%async_computation.5 | async-start | bytes 8192 | tf_op jit(solution)/shard_map/all_to_all | solution.py:141
Sparse Core Ops, SparseCore 0:
  117.5 32.8 all-gather.4
  174.7 17.1 all-gather.6

commit v3 on v2

--- a/solution.py
+++ b/solution.py
@@ -67,7 +67,9 @@
     quarter = slot_count // width
     destination = pack_dest[0]
 
-    info = lax.all_gather(jnp.concatenate([segment_ids, destination]), "rep", axis=0, tiled=False)
+    own_info = jnp.concatenate([segment_ids, destination])
+    copies = jnp.broadcast_to(own_info[None, :], (replicas, own_info.shape[0]))
+    info = lax.all_to_all(copies, "rep", split_axis=0, concat_axis=0, tiled=True)
     wide_ref = reference_rows.astype(jnp.float32)
     squares = lax.psum(jnp.sum(wide_ref * wide_ref, axis=1), "tp")
     own_inverse = jnp.sum(

time: 273 us -> 249 us (0.912)
  blocking collectives: 99.2 us -> 61.7 us
  waiting for transfers between devices: 87.5 us -> 98.4 us
  starting transfers between devices: 18.8 us -> 22.2 us
    unnamed x1 -> x0, blocking collectives: 37.5 us -> none
    all_to_all x1, waiting for transfers between devices: 0.01 us -> 5.76 us  [body(): lax.all_to_all(squares_sent, 'rep', split_axis=0, concat_axis=0, tiled=True)]
    all_to_all x0 -> x1, waiting for transfers between devices: none -> 5.18 us  [body(): lax.all_to_all(copies, 'rep', split_axis=0, concat_axis=0, tiled=True)]
    all_to_all x0 -> x1, starting transfers between devices: none -> 3.33 us  [body(): lax.all_to_all(copies, 'rep', split_axis=0, concat_axis=0, tiled=True)]
  transfers between devices with their start and end apart: 6 -> 7, of which waited for: 4 -> 6; matrix products, arithmetic and copies ran while one was open for 14% -> 15% of each run, Pallas kernels for 0% -> 0%
where the time goes in v3:
time: 249 us; the launch traced here: 248 us
  waiting for transfers between devices  98.4 us (40%)
  blocking collectives  61.7 us (25%)
  starting transfers between devices  22.2 us (9%)
  local copies, waits for them, and re-layouts  20.5 us (8%)
  matrix products  18.2 us (7%)
  between operations  14.4 us (6%)
  other arithmetic  12.3 us (5%)
    all_to_all x1, waiting for transfers between devices, body(): lax.all_to_all(partial, 'rep', split_axis=0, concat_axis=0, tiled=True)  38.2 us
    all_to_all x1, blocking collectives, body(): lax.all_to_all(split, 'rep', split_axis=1, concat_axis=0, tiled=True)  28.9 us
    all_gather x1, waiting for transfers between devices, body(): ref_slice = lax.all_gather(slices, 'tp', axis=0, tiled=True)  25.7 us
    all_to_all x1, blocking collectives, body(): lax.all_to_all(reference_rows, 'tp', split_axis=0, concat_axis=1, tiled=T...  17.9 us
    all_gather x1, waiting for transfers between devices, body(): critic_full = lax.all_gather(critic_in[chosen], 'tp', axis=1, tiled=True)  17.1 us
    dot_general x4, matrix products, project(): return jnp.dot(rows, weight, preferred_element_type=jnp.float32)  16.8 us
    gather x1, local copies, waits for them, and re-layouts, body(): compact = jnp.take(ref_slice, order, axis=0)  8.78 us
    psum x1, blocking collectives, body(): squares = lax.psum(jnp.sum(wide_ref * wide_ref, axis=1), 'tp')  8.31 us
  transfers between devices with their start and end apart: 7, of which 6 were waited for; matrix products, arithmetic and copies ran while one was open for 15% of the time, Pallas kernels for 0%

profile of v3, /device:TPU:0, one launch (start us, length us, event | category | flops | bytes accessed | tf_op | source)
XLA Modules:
  0.0 247.8 jit_solution(6949897502091696389)
XLA Ops:
  9.7 8.3 %psum.14 = f32[8,32]{1,0:T(8,128)S(1)} all-reduce(f32[8,32]{1,0:T(8,128)S(1)} %reshape.346), channel_id=1, replica_groups=mesh['rep'=8,'tp'=4] {'tp'}, use_global_device_ids=true, to_apply=%region_2.3 | all-reduce | flops 256 | bytes 2048 | tf_op jit(solution)/shard_map/psum | solution.py:74
  19.2 5.8 %all-to-all-start.1 = ((f32[8,1,32]{2,1,0:T(1,128)}), f32[8,1,32]{2,1,0:T(1,128)S(1)}, u32[]{:S(2)}, u32[]{:S(2)}) async-start(f32[8,1,32]{2,1,0:T(1,128)} %bitcast.4), calls=%async_computation.1 | async-start | bytes 8192 | tf_op jit(solution)/shard_map/all_to_all | solution.py:82
  25.8 5.8 %all-to-all-done.1 = f32[8,1,32]{2,1,0:T(1,128)S(1)} async-done(((f32[8,1,32]{2,1,0:T(1,128)}), f32[8,1,32]{2,1,0:T(1,128)S(1)}, u32[]{:S(2)}, u32[]{:S(2)}) %all-to-all-start.1) | async-done | bytes 1056 | tf_op jit(solution)/shard_map/all_to_all | solution.py:82
  32.1 3.3 %all-to-all-start = ((s32[8,1,264]{2,1,0:T(1,128)}), s32[8,1,264]{2,1,0:T(1,128)S(1)}, u32[]{:S(2)}, u32[]{:S(2)}) async-start(s32[8,1,264]{2,1,0:T(1,128)} %broadcast_in_dim.238), calls=%async_computation | async-start | bytes 24576 | tf_op jit(solution)/shard_map/all_to_all | solution.py:72
  36.8 5.2 %all-to-all-done = s32[8,1,264]{2,1,0:T(1,128)S(1)} async-done(((s32[8,1,264]{2,1,0:T(1,128)}), s32[8,1,264]{2,1,0:T(1,128)S(1)}, u32[]{:S(2)}, u32[]{:S(2)}) %all-to-all-start) | async-done | bytes 8480 | tf_op jit(solution)/shard_map/all_to_all | solution.py:72
  42.0 17.9 %all_to_all.77 = bf16[4,64,2048]{2,1,0:T(8,128)(2,1)S(1)} all-to-all(bf16[4,64,2048]{2,1,0:T(8,128)(2,1)} %bitcast.107), channel_id=1, replica_groups=mesh['rep'=8,'tp'=4] {'tp'}, dimensions={0} | all-to-all | bytes 2097152 | tf_op jit(solution)/shard_map/all_to_all | solution.py:87
  61.8 1.8 copy.103
  63.7 28.9 %all_to_all.78 = bf16[64,8,1024]{2,0,1:T(8,128)(2,1)} all-to-all(bf16[64,8,1024]{2,0,1:T(8,128)(2,1)S(1)} %copy.103), channel_id=1, replica_groups=mesh['rep'=8,'tp'=4] {'rep'}, dimensions={1} | all-to-all | bytes 2097152 | tf_op jit(solution)/shard_map/all_to_all | solution.py:88
  95.9 3.6 %all-to-all-start.5 = ((bf16[8,32,1024]{2,1,0:T(8,128)(2,1)}), bf16[8,32,1024]{2,1,0:T(8,128)(2,1)S(1)}, u32[]{:S(2)}, u32[]{:S(2)}) async-start(bf16[8,32,1024]{2,1,0:T(8,128)(2,1)} %broadcast_select_fusion), calls=%async_computation.5 | async-start | bytes 1048576 | tf_op jit(solution)/shard_map/all_to_all | solution.py:93
  99.9 25.7 %all-gather.4.cloned.1.call-done = bf16[2048,1024]{1,0:T(8,128)(2,1)} async-done(((bf16[512,1024]{1,0:T(8,128)(2,1)}), bf16[2048,1024]{1,0:T(8,128)(2,1)}) %all-gather.4.cloned.1.call-update) | async-done | bytes 4194320 | tf_op jit(solution)/shard_map/all_gather | solution.py:89
  125.6 8.8 %gather_fusion.1 = bf16[1024,1024]{1,0:T(8,128)(2,1)} fusion(bf16[2048,1024]{1,0:T(8,128)(2,1)} %all-gather.4.cloned.1.call-done, s32[1024]{0:T(1024)S(1)} %broadcast_clamp_fusion), kind=kCustom, calls=%fused_computation.1 | custom fusion | bytes 4198400 | tf_op jit(solution)/shard_map/jit(_take)/gather | solution.py:110
  134.4 7.7 %convolution_convert_fusion = bf16[1024,1536]{1,0:T(8,128)(2,1)} fusion(bf16[1024,256]{1,0:T(8,128)(2,1)} %param.18, bf16[1024,256]{1,0:T(8,128)(2,1)} %param.17, bf16[1024,1024]{1,0:T(8,128)(2,1)} %param.16, bf16[1024,1024]{1,0:T(8,128)(2,1)} %gather_fusion.1, pred[1024]{0:T(1024)(128)(4,1)S(1)} %compare_and_fusion), kind=kOutput, calls=%fused_computation.7 | convolution fusion | flops 3233284096 | bytes 8389632 | tf_op jit(solution)/shard_map/dot_general | solution.py:30
  142.0 5.5 %all-to-all-start.4 = ((bf16[8,128,1536]{2,1,0:T(8,128)(2,1)}), bf16[8,128,1536]{2,1,0:T(8,128)(2,1)}, u32[]{:S(2)}, u32[]{:S(2)}) async-start(bf16[8,128,1536]{2,1,0:T(8,128)(2,1)} %bitcast.110), calls=%async_computation.4 | async-start | bytes 6291456 | tf_op jit(solution)/shard_map/all_to_all | solution.py:113
  148.3 1.6 gather_fusion.3
  150.1 17.1 %all-gather.6.cloned.1.call-done = bf16[128,4096]{1,0:T(8,128)(2,1)} async-done(((bf16[128,1024]{1,0:T(8,128)(2,1)}), bf16[128,4096]{1,0:T(8,128)(2,1)}) %all-gather.6.cloned.1.call-update) | async-done | bytes 1048592 | tf_op jit(solution)/shard_map/all_gather | solution.py:115
  167.2 1.6 fusion.7
  168.9 1.7 convolution_convert_fusion.4
  170.6 4.7 %convolution_convert_fusion.2 = bf16[128,1024]{1,0:T(8,128)(2,1)S(1)} fusion(bf16[4096,1024]{1,0:T(8,128)(2,1)} %param.19, bf16[128,4096]{1,0:T(8,128)(2,1)S(1)} %copy-done.1, f32[128]{0:T(128)S(1)} %add_rsqrt_fusion), kind=kOutput, calls=%fused_computation.36 | convolution fusion | flops 1075445760 | bytes 9699840 | tf_op jit(solution)/shard_map/dot_general | solution.py:30
  176.2 2.7 %convolution_convert_fusion.5 = bf16[128,256]{1,0:T(8,128)(2,1)} fusion(bf16[4096,256]{1,0:T(8,128)(2,1)} %param.21, bf16[128,4096]{1,0:T(8,128)(2,1)S(1)} %copy-done.1, f32[128]{0:T(128)S(1)} %add_rsqrt_fusion), kind=kOutput, calls=%fused_computation.44 | convolution fusion | flops 270041088 | bytes 3211776 | tf_op jit(solution)/shard_map/dot_general | solution.py:30
  180.6 38.2 %all-to-all-done.4 = bf16[8,128,1536]{2,1,0:T(8,128)(2,1)} async-done(((bf16[8,128,1536]{2,1,0:T(8,128)(2,1)}), bf16[8,128,1536]{2,1,0:T(8,128)(2,1)}, u32[]{:S(2)}, u32[]{:S(2)}) %all-to-all-start.4) | async-done | bytes 3145760 | tf_op jit(solution)/shard_map/all_to_all | solution.py:113
  218.8 2.4 convert_reduce_fusion
  222.8 6.5 %psum.15 = f32[8,1,64]{2,0,1:T(8,128)} all-reduce(f32[8,1,64]{2,0,1:T(8,128)S(1)} %all_to_all.68), channel_id=1, replica_groups=mesh['rep'=8,'tp'=4] {'tp'}, use_global_device_ids=true, to_apply=%region_20.21 | all-reduce | flops 512 | bytes 4096 | tf_op jit(solution)/shard_map/psum | solution.py:141
  229.3 3.6 %all-to-all-start.6 = ((f32[8,1,64]{2,1,0:T(1,128)}), f32[8,1,64]{2,1,0:T(1,128)S(1)}, u32[]{:S(2)}, u32[]{:S(2)}) async-start(f32[8,1,64]{2,1,0:T(1,128)} %bitcast.41), calls=%async_computation.6 | async-start | bytes 8192 | tf_op jit(solution)/shard_map/all_to_all | solution.py:143
  232.9 6.4 %all-to-all-done.6 = f32[8,1,64]{2,1,0:T(1,128)S(1)} async-done(((f32[8,1,64]{2,1,0:T(1,128)}), f32[8,1,64]{2,1,0:T(1,128)S(1)}, u32[]{:S(2)}, u32[]{:S(2)}) %all-to-all-start.6) | async-done | bytes 2080 | tf_op jit(solution)/shard_map/all_to_all | solution.py:143
  (108 shorter events, 18.4 us)
Async XLA Ops:
  7.2 161.7 %copy-start = (bf16[4096,256]{1,0:T(8,128)(2,1)S(1)}, bf16[4096,256]{1,0:T(8,128)(2,1)}, u32[]{:S(2)}) copy-start(bf16[4096,256]{1,0:T(8,128)(2,1)} %param.20) | copy-start | bytes 6291460
  19.2 12.3 %all-to-all-start.1 = ((f32[8,1,32]{2,1,0:T(1,128)}), f32[8,1,32]{2,1,0:T(1,128)S(1)}, u32[]{:S(2)}, u32[]{:S(2)}) async-start(f32[8,1,32]{2,1,0:T(1,128)} %bitcast.4), calls=%async_computation.1 | async-start | bytes 8192 | tf_op jit(solution)/shard_map/all_to_all | solution.py:82
  32.1 9.8 %all-to-all-start = ((s32[8,1,264]{2,1,0:T(1,128)}), s32[8,1,264]{2,1,0:T(1,128)S(1)}, u32[]{:S(2)}, u32[]{:S(2)}) async-start(s32[8,1,264]{2,1,0:T(1,128)} %broadcast_in_dim.238), calls=%async_computation | async-start | bytes 24576 | tf_op jit(solution)/shard_map/all_to_all | solution.py:72
  35.5 90.1 %all-gather.4.cloned.1.call-start = ((), (), s32[]{:S(2)}) async-start(), calls=%async_computation.7 | async-start | bytes 5242880 | tf_op jit(solution)/shard_map/all_gather | solution.py:89
  63.6 30.7 %copy-start.2 = (bf16[256,1024]{1,0:T(8,128)(2,1)S(1)}, bf16[256,1024]{1,0:T(8,128)(2,1)}, u32[]{:S(2)}) copy-start(bf16[256,1024]{1,0:T(8,128)(2,1)} %param.13) | copy-start | bytes 1572868
  95.9 46.1 %all-to-all-start.5 = ((bf16[8,32,1024]{2,1,0:T(8,128)(2,1)}), bf16[8,32,1024]{2,1,0:T(8,128)(2,1)S(1)}, u32[]{:S(2)}, u32[]{:S(2)}) async-start(bf16[8,32,1024]{2,1,0:T(8,128)(2,1)} %broadcast_select_fusion), calls=%async_computation.5 | async-start | bytes 1048576 | tf_op jit(solution)/shard_map/all_to_all | solution.py:93
  142.0 76.7 %all-to-all-start.4 = ((bf16[8,128,1536]{2,1,0:T(8,128)(2,1)}), bf16[8,128,1536]{2,1,0:T(8,128)(2,1)}, u32[]{:S(2)}, u32[]{:S(2)}) async-start(bf16[8,128,1536]{2,1,0:T(8,128)(2,1)} %bitcast.110), calls=%async_computation.4 | async-start | bytes 6291456 | tf_op jit(solution)/shard_map/all_to_all | solution.py:113
  147.6 2.3 copy-start.4
  147.6 2.3 copy-start.5
  147.6 2.4 copy-start.7
  147.6 19.6 %all-gather.6.cloned.1.call-start = ((), (), s32[]{:S(2)}) async-start(), calls=%async_computation.8 | async-start | bytes 1310720 | tf_op jit(solution)/shard_map/all_gather | solution.py:115
  167.2 3.4 %copy-start.1 = (bf16[128,4096]{1,0:T(8,128)(2,1)S(1)}, bf16[128,4096]{1,0:T(8,128)(2,1)}, u32[]{:S(2)}) copy-start(bf16[128,4096]{1,0:T(8,128)(2,1)} %all-gather.6.cloned.1.call-done) | copy-start | bytes 3145732
  176.2 3.7 %copy-start.3 = (bf16[128,2,4,128]{3,2,1,0:T(4,128)(2,1)S(1)}, bf16[128,2,4,128]{3,2,1,0:T(4,128)(2,1)}, u32[]{:S(2)}) copy-start(bf16[128,2,4,128]{3,2,1,0:T(4,128)(2,1)} %reshape.358) | copy-start | bytes 786436
  221.4 11.6 %copy-start.6 = (s32[256]{0:T(256)S(1)}, s32[256]{0:T(256)}, u32[]{:S(2)}) copy-start(s32[256]{0:T(256)} %param.14) | copy-start | bytes 3076
  229.3 10.1 %all-to-all-start.6 = ((f32[8,1,64]{2,1,0:T(1,128)}), f32[8,1,64]{2,1,0:T(1,128)S(1)}, u32[]{:S(2)}, u32[]{:S(2)}) async-start(f32[8,1,64]{2,1,0:T(1,128)} %bitcast.41), calls=%async_computation.6 | async-start | bytes 8192 | tf_op jit(solution)/shard_map/all_to_all | solution.py:143
Sparse Core Ops, SparseCore 0:
  92.7 32.8 all-gather.3
  150.0 17.1 all-gather.5

commit v4 on v3

--- a/solution.py
+++ b/solution.py
@@ -80,9 +80,6 @@
     )
     squares_sent = jnp.take(squares.reshape(replicas, block_rows), own_inverse, axis=0)
     square_in = lax.all_to_all(squares_sent, "rep", split_axis=0, concat_axis=0, tiled=True).reshape(-1)
-    info, square_in, reference_rows, critic_rows = lax.optimization_barrier(
-        (info, square_in, reference_rows, critic_rows)
-    )
 
     split = lax.all_to_all(reference_rows, "tp", split_axis=0, concat_axis=1, tiled=True)
     slices = lax.all_to_all(split, "rep", split_axis=1, concat_axis=0, tiled=True)

time: 249 us -> 218 us (0.88)
  waiting for transfers between devices: 98.4 us -> 67.3 us
  other arithmetic: 12.3 us -> 9.62 us
    all_gather x1, waiting for transfers between devices: 25.7 us -> 2.35 us  [body(): ref_slice = lax.all_gather(slices, 'tp', axis=0, tiled=True)]
    all_to_all x1, waiting for transfers between devices: 5.18 us -> 0.01 us  [body(): lax.all_to_all(copies, 'rep', split_axis=0, concat_axis=0, tiled=True)]
    all_to_all x1, blocking collectives: 28.9 us -> 32 us  [body(): lax.all_to_all(split, 'rep', split_axis=1, concat_axis=0, tiled=True)]
  transfers between devices with their start and end apart: 7 -> 7, of which waited for: 6 -> 5; matrix products, arithmetic and copies ran while one was open for 15% -> 18% of each run, Pallas kernels for 0% -> 0%
where the time goes in v4:
time: 218 us; the launch traced here: 217 us
  waiting for transfers between devices  67.3 us (31%)
  blocking collectives  63.5 us (29%)
  starting transfers between devices  22.5 us (10%)
  local copies, waits for them, and re-layouts  21.6 us (10%)
  matrix products  18 us (8%)
  between operations  14.5 us (7%)
  other arithmetic  9.62 us (4%)
    all_to_all x1, waiting for transfers between devices, body(): lax.all_to_all(partial, 'rep', split_axis=0, concat_axis=0, tiled=True)  37 us
    all_to_all x1, blocking collectives, body(): lax.all_to_all(split, 'rep', split_axis=1, concat_axis=0, tiled=True)  32 us
    all_to_all x1, blocking collectives, body(): lax.all_to_all(reference_rows, 'tp', split_axis=0, concat_axis=1, tiled=T...  18.8 us
    all_gather x1, waiting for transfers between devices, body(): critic_full = lax.all_gather(critic_in[chosen], 'tp', axis=1, tiled=True)  17.2 us
    dot_general x4, matrix products, project(): return jnp.dot(rows, weight, preferred_element_type=jnp.float32)  16.7 us
    gather x1, local copies, waits for them, and re-layouts, body(): compact = jnp.take(ref_slice, order, axis=0)  8.78 us
    psum x1, blocking collectives, body(): spread = lax.psum(spread, 'tp').reshape(2, replicas, block_rows)  6.55 us
    all_to_all x1, waiting for transfers between devices, body(): back = lax.all_to_all(sent, 'rep', split_axis=0, concat_axis=0, tiled=True)  6.46 us
  transfers between devices with their start and end apart: 7, of which 5 were waited for; matrix products, arithmetic and copies ran while one was open for 18% of the time, Pallas kernels for 0%

profile of v4, /device:TPU:0, one launch (start us, length us, event | category | flops | bytes accessed | tf_op | source)
XLA Modules:
  0.0 216.9 jit_solution(6955402003224323287)
XLA Ops:
  7.2 18.8 %all_to_all.77 = bf16[4,64,2048]{2,1,0:T(8,128)(2,1)S(1)} all-to-all(bf16[4,64,2048]{2,1,0:T(8,128)(2,1)} %bitcast.107), channel_id=1, replica_groups=mesh['rep'=8,'tp'=4] {'tp'}, dimensions={0} | all-to-all | bytes 2097152 | tf_op jit(solution)/shard_map/all_to_all | solution.py:84
  28.0 1.8 copy.102
  29.8 32.0 %all_to_all.78 = bf16[64,8,1024]{2,0,1:T(8,128)(2,1)} all-to-all(bf16[64,8,1024]{2,0,1:T(8,128)(2,1)S(1)} %copy.102), channel_id=1, replica_groups=mesh['rep'=8,'tp'=4] {'rep'}, dimensions={1} | all-to-all | bytes 2097152 | tf_op jit(solution)/shard_map/all_to_all | solution.py:85
  62.5 3.5 %all-to-all-start = ((s32[8,1,264]{2,1,0:T(1,128)}), s32[8,1,264]{2,1,0:T(1,128)S(1)}, u32[]{:S(2)}, u32[]{:S(2)}) async-start(s32[8,1,264]{2,1,0:T(1,128)} %broadcast_in_dim.239), calls=%async_computation | async-start | bytes 24576 | tf_op jit(solution)/shard_map/all_to_all | solution.py:72
  66.4 6.1 %psum.14 = f32[8,32]{1,0:T(8,128)S(1)} all-reduce(f32[8,32]{1,0:T(8,128)S(1)} %reshape.347), channel_id=1, replica_groups=mesh['rep'=8,'tp'=4] {'tp'}, use_global_device_ids=true, to_apply=%region_8.9 | all-reduce | flops 256 | bytes 2048 | tf_op jit(solution)/shard_map/psum | solution.py:74
  73.2 1.6 gather_fusion.2
  76.5 6.0 %all-to-all-start.4 = ((f32[8,1,32]{2,1,0:T(1,128)}), f32[8,1,32]{2,1,0:T(1,128)S(1)}, u32[]{:S(2)}, u32[]{:S(2)}) async-start(f32[8,1,32]{2,1,0:T(1,128)} %bitcast.16), calls=%async_computation.4 | async-start | bytes 8192 | tf_op jit(solution)/shard_map/all_to_all | solution.py:82
  84.6 4.3 %all-to-all-done.4 = f32[8,1,32]{2,1,0:T(1,128)S(1)} async-done(((f32[8,1,32]{2,1,0:T(1,128)}), f32[8,1,32]{2,1,0:T(1,128)S(1)}, u32[]{:S(2)}, u32[]{:S(2)}) %all-to-all-start.4) | async-done | bytes 1056 | tf_op jit(solution)/shard_map/all_to_all | solution.py:82
  89.0 3.5 %all-to-all-start.5 = ((bf16[8,32,1024]{2,1,0:T(8,128)(2,1)}), bf16[8,32,1024]{2,1,0:T(8,128)(2,1)S(1)}, u32[]{:S(2)}, u32[]{:S(2)}) async-start(bf16[8,32,1024]{2,1,0:T(8,128)(2,1)} %broadcast_select_fusion), calls=%async_computation.5 | async-start | bytes 1048576 | tf_op jit(solution)/shard_map/all_to_all | solution.py:90
  92.5 2.4 %all-gather.4.cloned.1.call-done = bf16[2048,1024]{1,0:T(8,128)(2,1)} async-done(((bf16[512,1024]{1,0:T(8,128)(2,1)}), bf16[2048,1024]{1,0:T(8,128)(2,1)}) %all-gather.4.cloned.1.call-update) | async-done | bytes 4194320 | tf_op jit(solution)/shard_map/all_gather | solution.py:86
  94.9 8.8 %gather_fusion = bf16[1024,1024]{1,0:T(8,128)(2,1)} fusion(bf16[2048,1024]{1,0:T(8,128)(2,1)} %all-gather.4.cloned.1.call-done, s32[1024]{0:T(1024)S(1)} %broadcast_clamp_fusion), kind=kCustom, calls=%fused_computation | custom fusion | bytes 4198400 | tf_op jit(solution)/shard_map/jit(_take)/gather | solution.py:107
  103.6 7.5 %convolution_convert_fusion = bf16[1024,1536]{1,0:T(8,128)(2,1)} fusion(bf16[1024,256]{1,0:T(8,128)(2,1)S(1)} %copy-done.8, bf16[1024,256]{1,0:T(8,128)(2,1)} %param.17, bf16[1024,1024]{1,0:T(8,128)(2,1)} %param.16, bf16[1024,1024]{1,0:T(8,128)(2,1)} %gather_fusion, pred[1024]{0:T(1024)(128)(4,1)S(1)} %compare_and_fusion), kind=kOutput, calls=%fused_computation.7 | convolution fusion | flops 3233284096 | bytes 8389632 | tf_op jit(solution)/shard_map/dot_general | solution.py:30
  111.2 5.5 %all-to-all-start.3 = ((bf16[8,128,1536]{2,1,0:T(8,128)(2,1)}), bf16[8,128,1536]{2,1,0:T(8,128)(2,1)}, u32[]{:S(2)}, u32[]{:S(2)}) async-start(bf16[8,128,1536]{2,1,0:T(8,128)(2,1)} %bitcast.110), calls=%async_computation.3 | async-start | bytes 6291456 | tf_op jit(solution)/shard_map/all_to_all | solution.py:110
  118.7 1.6 gather_fusion.3
  120.5 17.2 %all-gather.6.cloned.1.call-done = bf16[128,4096]{1,0:T(8,128)(2,1)} async-done(((bf16[128,1024]{1,0:T(8,128)(2,1)}), bf16[128,4096]{1,0:T(8,128)(2,1)}) %all-gather.6.cloned.1.call-update) | async-done | bytes 1048592 | tf_op jit(solution)/shard_map/all_gather | solution.py:112
  137.6 1.6 fusion.7
  139.3 1.7 convolution_convert_fusion.4
  141.0 4.7 %convolution_convert_fusion.2 = bf16[128,1024]{1,0:T(8,128)(2,1)S(1)} fusion(bf16[4096,1024]{1,0:T(8,128)(2,1)} %param.19, bf16[128,4096]{1,0:T(8,128)(2,1)S(1)} %copy-done.1, f32[128]{0:T(128)S(1)} %add_rsqrt_fusion), kind=kOutput, calls=%fused_computation.36 | convolution fusion | flops 1075445760 | bytes 9699840 | tf_op jit(solution)/shard_map/dot_general | solution.py:30
  146.6 2.7 %convolution_convert_fusion.5 = bf16[128,256]{1,0:T(8,128)(2,1)} fusion(bf16[4096,256]{1,0:T(8,128)(2,1)} %param.21, bf16[128,4096]{1,0:T(8,128)(2,1)S(1)} %copy-done.1, f32[128]{0:T(128)S(1)} %add_rsqrt_fusion), kind=kOutput, calls=%fused_computation.44 | convolution fusion | flops 270041088 | bytes 3211776 | tf_op jit(solution)/shard_map/dot_general | solution.py:30
  150.9 37.0 %all-to-all-done.3 = bf16[8,128,1536]{2,1,0:T(8,128)(2,1)} async-done(((bf16[8,128,1536]{2,1,0:T(8,128)(2,1)}), bf16[8,128,1536]{2,1,0:T(8,128)(2,1)}, u32[]{:S(2)}, u32[]{:S(2)}) %all-to-all-start.3) | async-done | bytes 3145760 | tf_op jit(solution)/shard_map/all_to_all | solution.py:110
  187.9 2.4 %convert_reduce_fusion = f32[128,1536]{1,0:T(8,128)S(1)} fusion(bf16[8,128,1536]{2,1,0:T(8,128)(2,1)} %all-to-all-done.3), kind=kLoop, calls=%fused_computation.6 | loop fusion | flops 2949120 | bytes 3932160 | tf_op jit(solution)/shard_map/reduce_sum | solution.py:126
  191.9 6.5 %psum.15 = f32[8,1,64]{2,0,1:T(8,128)} all-reduce(f32[8,1,64]{2,0,1:T(8,128)S(1)} %all_to_all.68), channel_id=1, replica_groups=mesh['rep'=8,'tp'=4] {'tp'}, use_global_device_ids=true, to_apply=%region_20.21 | all-reduce | flops 512 | bytes 4096 | tf_op jit(solution)/shard_map/psum | solution.py:138
  198.5 3.6 %all-to-all-start.6 = ((f32[8,1,64]{2,1,0:T(1,128)}), f32[8,1,64]{2,1,0:T(1,128)S(1)}, u32[]{:S(2)}, u32[]{:S(2)}) async-start(f32[8,1,64]{2,1,0:T(1,128)} %bitcast.41), calls=%async_computation.6 | async-start | bytes 8192 | tf_op jit(solution)/shard_map/all_to_all | solution.py:140
  202.1 6.5 %all-to-all-done.6 = f32[8,1,64]{2,1,0:T(1,128)S(1)} async-done(((f32[8,1,64]{2,1,0:T(1,128)}), f32[8,1,64]{2,1,0:T(1,128)S(1)}, u32[]{:S(2)}, u32[]{:S(2)}) %all-to-all-start.6) | async-done | bytes 2080 | tf_op jit(solution)/shard_map/all_to_all | solution.py:140
  (110 shorter events, 15.1 us)
Async XLA Ops:
  7.2 132.1 %copy-start = (bf16[4096,256]{1,0:T(8,128)(2,1)S(1)}, bf16[4096,256]{1,0:T(8,128)(2,1)}, u32[]{:S(2)}) copy-start(bf16[4096,256]{1,0:T(8,128)(2,1)} %param.20) | copy-start | bytes 6291460
  7.2 87.7 %all-gather.4.cloned.1.call-start = ((), (), s32[]{:S(2)}) async-start(), calls=%async_computation.7 | async-start | bytes 5242880 | tf_op jit(solution)/shard_map/all_gather | solution.py:86
  29.8 32.1 %copy-start.6 = (s32[256]{0:T(256)S(1)}, s32[256]{0:T(256)}, u32[]{:S(2)}) copy-start(s32[256]{0:T(256)} %param.14) | copy-start | bytes 3076
  29.8 32.1 %copy-start.7 = (s32[1,8]{1,0:T(1,128)S(1)}, s32[1,8]{1,0:T(1,128)}, u32[]{:S(2)}) copy-start(s32[1,8]{1,0:T(1,128)} %param.15) | copy-start | bytes 100
  29.8 36.3 %copy-start.2 = (bf16[256,2048]{1,0:T(8,128)(2,1)S(1)}, bf16[256,2048]{1,0:T(8,128)(2,1)}, u32[]{:S(2)}) copy-start(bf16[256,2048]{1,0:T(8,128)(2,1)} %param.12) | copy-start | bytes 3145732
  62.5 14.0 %all-to-all-start = ((s32[8,1,264]{2,1,0:T(1,128)}), s32[8,1,264]{2,1,0:T(1,128)S(1)}, u32[]{:S(2)}, u32[]{:S(2)}) async-start(s32[8,1,264]{2,1,0:T(1,128)} %broadcast_in_dim.239), calls=%async_computation | async-start | bytes 24576 | tf_op jit(solution)/shard_map/all_to_all | solution.py:72
  76.5 12.5 %all-to-all-start.4 = ((f32[8,1,32]{2,1,0:T(1,128)}), f32[8,1,32]{2,1,0:T(1,128)S(1)}, u32[]{:S(2)}, u32[]{:S(2)}) async-start(f32[8,1,32]{2,1,0:T(1,128)} %bitcast.16), calls=%async_computation.4 | async-start | bytes 8192 | tf_op jit(solution)/shard_map/all_to_all | solution.py:82
  89.0 22.2 %all-to-all-start.5 = ((bf16[8,32,1024]{2,1,0:T(8,128)(2,1)}), bf16[8,32,1024]{2,1,0:T(8,128)(2,1)S(1)}, u32[]{:S(2)}, u32[]{:S(2)}) async-start(bf16[8,32,1024]{2,1,0:T(8,128)(2,1)} %broadcast_select_fusion), calls=%async_computation.5 | async-start | bytes 1048576 | tf_op jit(solution)/shard_map/all_to_all | solution.py:90
  92.5 11.1 %copy-start.8 = (bf16[1024,256]{1,0:T(8,128)(2,1)S(1)}, bf16[1024,256]{1,0:T(8,128)(2,1)}, u32[]{:S(2)}) copy-start(bf16[1024,256]{1,0:T(8,128)(2,1)} %param.18) | copy-start | bytes 1572868
  111.2 76.7 %all-to-all-start.3 = ((bf16[8,128,1536]{2,1,0:T(8,128)(2,1)}), bf16[8,128,1536]{2,1,0:T(8,128)(2,1)}, u32[]{:S(2)}, u32[]{:S(2)}) async-start(bf16[8,128,1536]{2,1,0:T(8,128)(2,1)} %bitcast.110), calls=%async_computation.3 | async-start | bytes 6291456 | tf_op jit(solution)/shard_map/all_to_all | solution.py:110
  116.7 3.6 %copy-start.4 = (bf16[1024]{0:T(1024)(128)(2,1)S(1)}, bf16[1024]{0:T(1024)(128)(2,1)}, u32[]{:S(2)}) copy-start(bf16[1024]{0:T(1024)(128)(2,1)} %param.22) | copy-start | bytes 6148
  116.7 3.6 %copy-start.5 = (bf16[1024]{0:T(1024)(128)(2,1)S(1)}, bf16[1024]{0:T(1024)(128)(2,1)}, u32[]{:S(2)}) copy-start(bf16[1024]{0:T(1024)(128)(2,1)} %param.23) | copy-start | bytes 6148
  116.7 20.9 %all-gather.6.cloned.1.call-start = ((), (), s32[]{:S(2)}) async-start(), calls=%async_computation.8 | async-start | bytes 1310720 | tf_op jit(solution)/shard_map/all_gather | solution.py:112
  137.6 3.4 %copy-start.1 = (bf16[128,4096]{1,0:T(8,128)(2,1)S(1)}, bf16[128,4096]{1,0:T(8,128)(2,1)}, u32[]{:S(2)}) copy-start(bf16[128,4096]{1,0:T(8,128)(2,1)} %all-gather.6.cloned.1.call-done) | copy-start | bytes 3145732
  146.6 3.7 %copy-start.3 = (bf16[128,2,4,128]{3,2,1,0:T(4,128)(2,1)S(1)}, bf16[128,2,4,128]{3,2,1,0:T(4,128)(2,1)}, u32[]{:S(2)}) copy-start(bf16[128,2,4,128]{3,2,1,0:T(4,128)(2,1)} %reshape.354) | copy-start | bytes 786436
  198.5 10.1 %all-to-all-start.6 = ((f32[8,1,64]{2,1,0:T(1,128)}), f32[8,1,64]{2,1,0:T(1,128)S(1)}, u32[]{:S(2)}, u32[]{:S(2)}) async-start(f32[8,1,64]{2,1,0:T(1,128)} %bitcast.41), calls=%async_computation.6 | async-start | bytes 8192 | tf_op jit(solution)/shard_map/all_to_all | solution.py:140
Sparse Core Ops, SparseCore 0:
  62.0 32.8 all-gather.3
  120.4 17.2 all-gather.5

commit v5 on v4

--- a/solution.py
+++ b/solution.py
@@ -104,7 +104,8 @@
     chosen = jnp.sum(jnp.where(place_mine, position[None, :], 0), axis=1)
     pack_ids = jnp.sum(jnp.where(place_mine, mine(received)[None, :], 0), axis=1)
 
-    compact = jnp.take(ref_slice, order, axis=0)
+    pick = (order[:, None] == jnp.arange(ref_slice.shape[0])[None, :]).astype(jnp.bfloat16)
+    compact = project(pick, ref_slice).astype(jnp.bfloat16)
     weight = jnp.concatenate([ref_query, ref_key, ref_value], axis=1)
     partial = project(compact, weight).astype(jnp.bfloat16)
     parts = lax.all_to_all(partial, "rep", split_axis=0, concat_axis=0, tiled=True)

time: 218 us -> 214 us (0.982)
  local copies, waits for them, and re-layouts: 21.6 us -> 12.8 us
  matrix products: 18 us -> 22.8 us
    gather x1 -> x0, local copies, waits for them, and re-layouts: 8.78 us -> none  [body(): compact = jnp.take(ref_slice, order, axis=0)]
    dot_general x4 -> x5, matrix products: 16.7 us -> 21.4 us  [project(): return jnp.dot(rows, weight, preferred_element_type=jnp.float32)]
  transfers between devices with their start and end apart: 7 -> 7, of which waited for: 5 -> 5; matrix products, arithmetic and copies ran while one was open for 18% -> 17% of each run, Pallas kernels for 0% -> 0%
where the time goes in v5:
time: 214 us; the launch traced here: 213 us
  waiting for transfers between devices  67.4 us (31%)
  blocking collectives  63.5 us (30%)
  matrix products  22.8 us (11%)
  starting transfers between devices  22.5 us (11%)
  between operations  14.5 us (7%)
  local copies, waits for them, and re-layouts  12.8 us (6%)
  other arithmetic  9.59 us (4%)
    all_to_all x1, waiting for transfers between devices, body(): lax.all_to_all(partial, 'rep', split_axis=0, concat_axis=0, tiled=True)  37 us
    all_to_all x1, blocking collectives, body(): lax.all_to_all(split, 'rep', split_axis=1, concat_axis=0, tiled=True)  32 us
    dot_general x5, matrix products, project(): return jnp.dot(rows, weight, preferred_element_type=jnp.float32)  21.4 us
    all_to_all x1, blocking collectives, body(): lax.all_to_all(reference_rows, 'tp', split_axis=0, concat_axis=1, tiled=T...  18.8 us
    all_gather x1, waiting for transfers between devices, body(): critic_full = lax.all_gather(critic_in[chosen], 'tp', axis=1, tiled=True)  17.2 us
    psum x1, blocking collectives, body(): spread = lax.psum(spread, 'tp').reshape(2, replicas, block_rows)  6.53 us
    all_to_all x1, waiting for transfers between devices, body(): back = lax.all_to_all(sent, 'rep', split_axis=0, concat_axis=0, tiled=True)  6.46 us
    psum x1, blocking collectives, body(): squares = lax.psum(jnp.sum(wide_ref * wide_ref, axis=1), 'tp')  6.07 us
  transfers between devices with their start and end apart: 7, of which 5 were waited for; matrix products, arithmetic and copies ran while one was open for 17% of the time, Pallas kernels for 0%

profile of v5, /device:TPU:0, one launch (start us, length us, event | category | flops | bytes accessed | tf_op | source)
XLA Modules:
  0.0 213.0 jit_solution(10816725883397479566)
XLA Ops:
  7.2 18.8 %all_to_all.77 = bf16[4,64,2048]{2,1,0:T(8,128)(2,1)S(1)} all-to-all(bf16[4,64,2048]{2,1,0:T(8,128)(2,1)} %bitcast.104), channel_id=1, replica_groups=mesh['rep'=8,'tp'=4] {'tp'}, dimensions={0} | all-to-all | bytes 2097152 | tf_op jit(solution)/shard_map/all_to_all | solution.py:84
  28.0 1.8 copy.102
  29.8 32.0 %all_to_all.78 = bf16[64,8,1024]{2,0,1:T(8,128)(2,1)} all-to-all(bf16[64,8,1024]{2,0,1:T(8,128)(2,1)S(1)} %copy.102), channel_id=1, replica_groups=mesh['rep'=8,'tp'=4] {'rep'}, dimensions={1} | all-to-all | bytes 2097152 | tf_op jit(solution)/shard_map/all_to_all | solution.py:85
  62.5 3.5 %all-to-all-start = ((s32[8,1,264]{2,1,0:T(1,128)}), s32[8,1,264]{2,1,0:T(1,128)S(1)}, u32[]{:S(2)}, u32[]{:S(2)}) async-start(s32[8,1,264]{2,1,0:T(1,128)} %broadcast_in_dim.230), calls=%async_computation | async-start | bytes 24576 | tf_op jit(solution)/shard_map/all_to_all | solution.py:72
  66.4 6.1 %psum.14 = f32[8,32]{1,0:T(8,128)S(1)} all-reduce(f32[8,32]{1,0:T(8,128)S(1)} %reshape.307), channel_id=1, replica_groups=mesh['rep'=8,'tp'=4] {'tp'}, use_global_device_ids=true, to_apply=%region_8.9 | all-reduce | flops 256 | bytes 2048 | tf_op jit(solution)/shard_map/psum | solution.py:74
  73.2 1.6 gather_fusion.1
  76.5 6.0 %all-to-all-start.4 = ((f32[8,1,32]{2,1,0:T(1,128)}), f32[8,1,32]{2,1,0:T(1,128)S(1)}, u32[]{:S(2)}, u32[]{:S(2)}) async-start(f32[8,1,32]{2,1,0:T(1,128)} %bitcast.14), calls=%async_computation.4 | async-start | bytes 8192 | tf_op jit(solution)/shard_map/all_to_all | solution.py:82
  84.6 4.4 %all-to-all-done.4 = f32[8,1,32]{2,1,0:T(1,128)S(1)} async-done(((f32[8,1,32]{2,1,0:T(1,128)}), f32[8,1,32]{2,1,0:T(1,128)S(1)}, u32[]{:S(2)}, u32[]{:S(2)}) %all-to-all-start.4) | async-done | bytes 1056 | tf_op jit(solution)/shard_map/all_to_all | solution.py:82
  89.0 3.5 %all-to-all-start.5 = ((bf16[8,32,1024]{2,1,0:T(8,128)(2,1)}), bf16[8,32,1024]{2,1,0:T(8,128)(2,1)S(1)}, u32[]{:S(2)}, u32[]{:S(2)}) async-start(bf16[8,32,1024]{2,1,0:T(8,128)(2,1)} %broadcast_select_fusion), calls=%async_computation.5 | async-start | bytes 1048576 | tf_op jit(solution)/shard_map/all_to_all | solution.py:90
  92.5 2.4 %all-gather.4.cloned.1.call-done = bf16[2048,1024]{1,0:T(8,128)(2,1)} async-done(((bf16[512,1024]{1,0:T(8,128)(2,1)}), bf16[2048,1024]{1,0:T(8,128)(2,1)}) %all-gather.4.cloned.1.call-update) | async-done | bytes 4194320 | tf_op jit(solution)/shard_map/all_gather | solution.py:86
  94.9 7.2 %fusion.2 = bf16[1024,1024]{1,0:T(8,128)(2,1)S(1)} fusion(bf16[2048,1024]{1,0:T(8,128)(2,1)} %all-gather.4.cloned.1.call-done, s32[1024]{0:T(1024)S(1)} %bitcast.120), kind=kOutput, calls=%fused_computation.6 | convolution fusion | flops 4297064448 | bytes 6295552 | tf_op jit(solution)/shard_map/dot_general | solution.py:30
  102.1 5.1 %convolution_convert_fusion = bf16[1024,1536]{1,0:T(8,128)(2,1)} fusion(bf16[1024,256]{1,0:T(8,128)(2,1)S(1)} %copy-done.9, bf16[1024,256]{1,0:T(8,128)(2,1)S(1)} %copy-done.10, bf16[1024,1024]{1,0:T(8,128)(2,1)S(1)} %copy-done.8, bf16[1024,1024]{1,0:T(8,128)(2,1)S(1)} %fusion.2), kind=kOutput, calls=%fused_computation.9 | convolution fusion | flops 3232235520 | bytes 8388608 | tf_op jit(solution)/shard_map/dot_general | solution.py:30
  107.2 5.5 %all-to-all-start.3 = ((bf16[8,128,1536]{2,1,0:T(8,128)(2,1)}), bf16[8,128,1536]{2,1,0:T(8,128)(2,1)}, u32[]{:S(2)}, u32[]{:S(2)}) async-start(bf16[8,128,1536]{2,1,0:T(8,128)(2,1)} %bitcast.107), calls=%async_computation.3 | async-start | bytes 6291456 | tf_op jit(solution)/shard_map/all_to_all | solution.py:111
  114.7 1.6 gather_fusion.2
  116.5 17.2 %all-gather.6.cloned.1.call-done = bf16[128,4096]{1,0:T(8,128)(2,1)} async-done(((bf16[128,1024]{1,0:T(8,128)(2,1)}), bf16[128,4096]{1,0:T(8,128)(2,1)}) %all-gather.6.cloned.1.call-update) | async-done | bytes 1048592 | tf_op jit(solution)/shard_map/all_gather | solution.py:113
  133.7 1.6 fusion.9
  135.3 1.7 convolution_convert_fusion.4
  137.1 4.7 %convolution_convert_fusion.2 = bf16[128,1024]{1,0:T(8,128)(2,1)S(1)} fusion(bf16[4096,1024]{1,0:T(8,128)(2,1)} %param.19, bf16[128,4096]{1,0:T(8,128)(2,1)S(1)} %copy-done.1, f32[128]{0:T(128)S(1)} %add_rsqrt_fusion), kind=kOutput, calls=%fused_computation.37 | convolution fusion | flops 1075445760 | bytes 9699840 | tf_op jit(solution)/shard_map/dot_general | solution.py:30
  142.6 2.7 %convolution_convert_fusion.5 = bf16[128,256]{1,0:T(8,128)(2,1)} fusion(bf16[4096,256]{1,0:T(8,128)(2,1)} %param.21, bf16[128,4096]{1,0:T(8,128)(2,1)S(1)} %copy-done.1, f32[128]{0:T(128)S(1)} %add_rsqrt_fusion), kind=kOutput, calls=%fused_computation.45 | convolution fusion | flops 270041088 | bytes 3211776 | tf_op jit(solution)/shard_map/dot_general | solution.py:30
  147.0 37.0 %all-to-all-done.3 = bf16[8,128,1536]{2,1,0:T(8,128)(2,1)} async-done(((bf16[8,128,1536]{2,1,0:T(8,128)(2,1)}), bf16[8,128,1536]{2,1,0:T(8,128)(2,1)}, u32[]{:S(2)}, u32[]{:S(2)}) %all-to-all-start.3) | async-done | bytes 3145760 | tf_op jit(solution)/shard_map/all_to_all | solution.py:111
  184.0 2.4 %convert_reduce_fusion = f32[128,1536]{1,0:T(8,128)S(1)} fusion(bf16[8,128,1536]{2,1,0:T(8,128)(2,1)} %all-to-all-done.3), kind=kLoop, calls=%fused_computation.7 | loop fusion | flops 2949120 | bytes 3932160 | tf_op jit(solution)/shard_map/reduce_sum | solution.py:127
  188.0 6.5 %psum.15 = f32[8,1,64]{2,0,1:T(8,128)} all-reduce(f32[8,1,64]{2,0,1:T(8,128)S(1)} %all_to_all.68), channel_id=1, replica_groups=mesh['rep'=8,'tp'=4] {'tp'}, use_global_device_ids=true, to_apply=%region_20.21 | all-reduce | flops 512 | bytes 4096 | tf_op jit(solution)/shard_map/psum | solution.py:139
  194.5 3.6 %all-to-all-start.6 = ((f32[8,1,64]{2,1,0:T(1,128)}), f32[8,1,64]{2,1,0:T(1,128)S(1)}, u32[]{:S(2)}, u32[]{:S(2)}) async-start(f32[8,1,64]{2,1,0:T(1,128)} %bitcast.39), calls=%async_computation.6 | async-start | bytes 8192 | tf_op jit(solution)/shard_map/all_to_all | solution.py:141
  198.1 6.5 %all-to-all-done.6 = f32[8,1,64]{2,1,0:T(1,128)S(1)} async-done(((f32[8,1,64]{2,1,0:T(1,128)}), f32[8,1,64]{2,1,0:T(1,128)S(1)}, u32[]{:S(2)}, u32[]{:S(2)}) %all-to-all-start.6) | async-done | bytes 2080 | tf_op jit(solution)/shard_map/all_to_all | solution.py:141
  (111 shorter events, 15.0 us)
Async XLA Ops:
  7.2 128.1 %copy-start = (bf16[4096,256]{1,0:T(8,128)(2,1)S(1)}, bf16[4096,256]{1,0:T(8,128)(2,1)}, u32[]{:S(2)}) copy-start(bf16[4096,256]{1,0:T(8,128)(2,1)} %param.20) | copy-start | bytes 6291460
  7.2 87.7 %all-gather.4.cloned.1.call-start = ((), (), s32[]{:S(2)}) async-start(), calls=%async_computation.7 | async-start | bytes 5242880 | tf_op jit(solution)/shard_map/all_gather | solution.py:86
  29.8 32.1 %copy-start.6 = (s32[256]{0:T(256)S(1)}, s32[256]{0:T(256)}, u32[]{:S(2)}) copy-start(s32[256]{0:T(256)} %param.14) | copy-start | bytes 3076
  29.8 32.1 %copy-start.7 = (s32[1,8]{1,0:T(1,128)S(1)}, s32[1,8]{1,0:T(1,128)}, u32[]{:S(2)}) copy-start(s32[1,8]{1,0:T(1,128)} %param.15) | copy-start | bytes 100
  29.8 36.3 %copy-start.2 = (bf16[256,2048]{1,0:T(8,128)(2,1)S(1)}, bf16[256,2048]{1,0:T(8,128)(2,1)}, u32[]{:S(2)}) copy-start(bf16[256,2048]{1,0:T(8,128)(2,1)} %param.12) | copy-start | bytes 3145732
  62.5 14.0 %all-to-all-start = ((s32[8,1,264]{2,1,0:T(1,128)}), s32[8,1,264]{2,1,0:T(1,128)S(1)}, u32[]{:S(2)}, u32[]{:S(2)}) async-start(s32[8,1,264]{2,1,0:T(1,128)} %broadcast_in_dim.230), calls=%async_computation | async-start | bytes 24576 | tf_op jit(solution)/shard_map/all_to_all | solution.py:72
  76.5 12.5 %all-to-all-start.4 = ((f32[8,1,32]{2,1,0:T(1,128)}), f32[8,1,32]{2,1,0:T(1,128)S(1)}, u32[]{:S(2)}, u32[]{:S(2)}) async-start(f32[8,1,32]{2,1,0:T(1,128)} %bitcast.14), calls=%async_computation.4 | async-start | bytes 8192 | tf_op jit(solution)/shard_map/all_to_all | solution.py:82
  89.0 18.2 %all-to-all-start.5 = ((bf16[8,32,1024]{2,1,0:T(8,128)(2,1)}), bf16[8,32,1024]{2,1,0:T(8,128)(2,1)S(1)}, u32[]{:S(2)}, u32[]{:S(2)}) async-start(bf16[8,32,1024]{2,1,0:T(8,128)(2,1)} %broadcast_select_fusion), calls=%async_computation.5 | async-start | bytes 1048576 | tf_op jit(solution)/shard_map/all_to_all | solution.py:90
  94.9 7.2 %copy-start.8 = (bf16[1024,1024]{1,0:T(8,128)(2,1)S(1)}, bf16[1024,1024]{1,0:T(8,128)(2,1)}, u32[]{:S(2)}) copy-start(bf16[1024,1024]{1,0:T(8,128)(2,1)} %param.16) | copy-start | bytes 6291460
  94.9 7.2 %copy-start.9 = (bf16[1024,256]{1,0:T(8,128)(2,1)S(1)}, bf16[1024,256]{1,0:T(8,128)(2,1)}, u32[]{:S(2)}) copy-start(bf16[1024,256]{1,0:T(8,128)(2,1)} %param.18) | copy-start | bytes 1572868
  94.9 7.2 %copy-start.10 = (bf16[1024,256]{1,0:T(8,128)(2,1)S(1)}, bf16[1024,256]{1,0:T(8,128)(2,1)}, u32[]{:S(2)}) copy-start(bf16[1024,256]{1,0:T(8,128)(2,1)} %param.17) | copy-start | bytes 1572868
  107.2 76.7 %all-to-all-start.3 = ((bf16[8,128,1536]{2,1,0:T(8,128)(2,1)}), bf16[8,128,1536]{2,1,0:T(8,128)(2,1)}, u32[]{:S(2)}, u32[]{:S(2)}) async-start(bf16[8,128,1536]{2,1,0:T(8,128)(2,1)} %bitcast.107), calls=%async_computation.3 | async-start | bytes 6291456 | tf_op jit(solution)/shard_map/all_to_all | solution.py:111
  112.7 3.6 %copy-start.4 = (bf16[1024]{0:T(1024)(128)(2,1)S(1)}, bf16[1024]{0:T(1024)(128)(2,1)}, u32[]{:S(2)}) copy-start(bf16[1024]{0:T(1024)(128)(2,1)} %param.22) | copy-start | bytes 6148
  112.7 3.6 %copy-start.5 = (bf16[1024]{0:T(1024)(128)(2,1)S(1)}, bf16[1024]{0:T(1024)(128)(2,1)}, u32[]{:S(2)}) copy-start(bf16[1024]{0:T(1024)(128)(2,1)} %param.23) | copy-start | bytes 6148
  112.8 20.9 %all-gather.6.cloned.1.call-start = ((), (), s32[]{:S(2)}) async-start(), calls=%async_computation.8 | async-start | bytes 1310720 | tf_op jit(solution)/shard_map/all_gather | solution.py:113
  133.7 3.4 %copy-start.1 = (bf16[128,4096]{1,0:T(8,128)(2,1)S(1)}, bf16[128,4096]{1,0:T(8,128)(2,1)}, u32[]{:S(2)}) copy-start(bf16[128,4096]{1,0:T(8,128)(2,1)} %all-gather.6.cloned.1.call-done) | copy-start | bytes 3145732
  142.6 3.7 %copy-start.3 = (bf16[128,2,4,128]{3,2,1,0:T(4,128)(2,1)S(1)}, bf16[128,2,4,128]{3,2,1,0:T(4,128)(2,1)}, u32[]{:S(2)}) copy-start(bf16[128,2,4,128]{3,2,1,0:T(4,128)(2,1)} %reshape.314) | copy-start | bytes 786436
  194.5 10.1 %all-to-all-start.6 = ((f32[8,1,64]{2,1,0:T(1,128)}), f32[8,1,64]{2,1,0:T(1,128)S(1)}, u32[]{:S(2)}, u32[]{:S(2)}) async-start(f32[8,1,64]{2,1,0:T(1,128)} %bitcast.39), calls=%async_computation.6 | async-start | bytes 8192 | tf_op jit(solution)/shard_map/all_to_all | solution.py:141
Sparse Core Ops, SparseCore 0:
  62.0 32.8 all-gather.3
  116.4 17.2 all-gather.5
